TPU v7x, 512 devices: a whole 4x8x8 slice. The times are simulated.
512 devices in a mesh: member: 16 (over z, x_hi), lat: 4 (over x_lo, core), lon: 8 (over y).
Axes of the slice: x: 4 (x_hi: 2, x_lo: 2; x = x_hi * 2 + x_lo), y: 8, z: 8, core: 2. Of those that a mesh axis runs over, the one named last changes fastest.
Arguments:
- inputs: bfloat16 [16, 16, 64, 1024], P('member', None, 'lat', 'lon'), may hold values from -6 to 6
- target: bfloat16 [16, 64, 1024], P(None, 'lat', 'lon'), may hold values from -6 to 6
- conv_in: bfloat16 [9, 128, 16], replicated, may hold values from -0.5 to 0.5
- bias_in: float32 [128], replicated, may hold values from -3 to 3
- conv_out: bfloat16 [9, 16, 128], replicated, may hold values from -0.1875 to 0.1875
Outputs:
- input_grad: float32 [16, 16, 64, 1024], P('member', None, 'lat', 'lon')
- conv_in_grad: float32 [9, 128, 16], replicated
- conv_out_grad: float32 [9, 16, 128], replicated
All inputs are finite; a program needn't handle non-finite values.
Results may differ from a plain program's by a relative error of at most 0.013.
Values may be sent and summed in bfloat16 or wider, within the bound.
A program may use at most 64 MiB of HBM per device.

v0:
```python
import math

import jax
import jax.numpy as jnp
from jax import lax
from jax.sharding import PartitionSpec as P


def extended(cells, sides, width):
    for axis, dim in sides:
        count = lax.axis_size(axis)
        head = lax.slice_in_dim(cells, 0, width, axis=dim)
        tail = lax.slice_in_dim(cells, cells.shape[dim] - width, cells.shape[dim], axis=dim)
        cells = jnp.concatenate(
            [
                lax.ppermute(tail, axis, [(i, (i + 1) % count) for i in range(count)]),
                cells,
                lax.ppermute(head, axis, [((i + 1) % count, i) for i in range(count)]),
            ],
            axis=dim,
        )
    return cells


def kernel_slope(difference):
    return difference / jnp.sqrt(difference * difference + 0.25)


def silu_slope(hidden_pre):
    sigmoid = jax.nn.sigmoid(hidden_pre)
    return sigmoid * (1.0 + hidden_pre * (1.0 - sigmoid))


def stencil_at(weight, padded, anchor, flip, row_count, col_count):
    running = None
    for row_step in (-1, 0, 1):
        for col_step in (-1, 0, 1):
            offset = 3 * (row_step + 1) + (col_step + 1)
            matrix = weight[offset] if flip == 1 else weight[offset].T
            start_row = anchor + flip * row_step
            start_col = anchor + flip * col_step
            window = padded[:, start_row : start_row + row_count, start_col : start_col + col_count]
            window = window.reshape(padded.shape[0], row_count * col_count)
            term = jnp.dot(matrix, window, preferred_element_type=jnp.float32)
            running = term if running is None else running + term
    return running.reshape(-1, row_count, col_count)


def shards(inputs, target, conv_in, bias_in, conv_out):
    members = lax.axis_size("member")
    lat_count = lax.axis_size("lat")
    lon_count = lax.axis_size("lon")
    field = inputs[0]
    levels, tile_rows, tile_cols = field.shape
    grid_rows = tile_rows * lat_count
    row_index = lax.axis_index("lat") * tile_rows + jnp.arange(-2, tile_rows + 2)
    inside_two = (row_index >= 0) & (row_index < grid_rows)
    inside_one = inside_two[1:-1]
    padded_in = extended(field, (("lat", 1), ("lon", 2)), 2)
    padded_in = jnp.where(inside_two[None, :, None], padded_in, jnp.zeros_like(padded_in))
    hidden_pre = (
        stencil_at(conv_in, padded_in, 1, 1, tile_rows + 2, tile_cols + 2) + bias_in[:, None, None]
    )
    activated = jnp.where(inside_one[None, :, None], jax.nn.silu(hidden_pre), 0.0).astype(
        jnp.bfloat16
    )
    summed = field.astype(jnp.float32) + stencil_at(conv_out, activated, 1, 1, tile_rows, tile_cols)
    prediction = summed.astype(jnp.bfloat16)
    own_pred = prediction.astype(jnp.float32)
    coupling = (1.0 - 0.05 / members) / (members - 1)
    target_wide = target.astype(jnp.float32)
    difference = own_pred[None] - lax.all_gather(
        prediction[None], "member", axis=0, tiled=True
    ).astype(jnp.float32)
    spread = jnp.sum(kernel_slope(difference), axis=0)
    grad_pred = (kernel_slope(own_pred - target_wide) - coupling * spread).astype(jnp.bfloat16)
    padded_grad = extended(grad_pred, (("lat", 1), ("lon", 2)), 2)
    padded_grad = jnp.where(inside_two[None, :, None], padded_grad, jnp.zeros_like(padded_grad))
    grad_act = stencil_at(conv_out, padded_grad, 1, -1, tile_rows + 2, tile_cols + 2)
    grad_hidden = jnp.where(
        inside_one[None, :, None], grad_act * silu_slope(hidden_pre), 0.0
    ).astype(jnp.bfloat16)
    grad_field = grad_pred.astype(jnp.float32) + stencil_at(
        conv_in, grad_hidden, 1, -1, tile_rows, tile_cols
    )
    flat_hidden = grad_hidden[:, 1:-1, 1:-1].reshape(grad_hidden.shape[0], -1)
    flat_pred = grad_pred.reshape(levels, -1)
    in_terms = []
    out_terms = []
    for row_step in (-1, 0, 1):
        for col_step in (-1, 0, 1):
            in_window = padded_in[
                :, 2 + row_step : 2 + row_step + tile_rows, 2 + col_step : 2 + col_step + tile_cols
            ]
            act_window = activated[
                :, 1 + row_step : 1 + row_step + tile_rows, 1 + col_step : 1 + col_step + tile_cols
            ]
            in_window = in_window.reshape(levels, -1)
            act_window = act_window.reshape(act_window.shape[0], -1)
            in_terms.append(jnp.dot(flat_hidden, in_window.T, preferred_element_type=jnp.float32))
            out_terms.append(jnp.dot(flat_pred, act_window.T, preferred_element_type=jnp.float32))
    in_total, out_total = lax.psum(
        (jnp.stack(in_terms), jnp.stack(out_terms)), ("member", "lat", "lon")
    )
    scale = 1.0 / math.sqrt(members * grid_rows * tile_cols * lon_count)
    return (grad_field[None], in_total * scale, out_total * scale)


def solution(mesh):
    in_specs = (P("member", None, "lat", "lon"), P(None, "lat", "lon"), P(), P(), P())
    out_specs = (P("member", None, "lat", "lon"), P(), P())
    return jax.shard_map(shards, mesh=mesh, in_specs=in_specs, out_specs=out_specs, check_vma=False)
```

profile of v0, /device:TPU:1, one launch (start us, length us, event | category | flops | bytes accessed | tf_op | source)
XLA Modules:
  0.0 482.0 jit_solution(10419521597159083449)
XLA Ops:
  8.1 4.5 collective-permute-start
  12.6 6.2 %collective-permute-start.1 = (bf16[16,2,128]{2,0,1:T(8,128)(2,1)S(1)}, bf16[16,2,128]{2,0,1:T(8,128)(2,1)S(1)}, u32[]{:S(2)}, u32[]{:S(2)}) collective-permute-start(bf16[16,2,128]{2,0,1:T(8,128)(2,1)S(1)} %get-tuple-element.59), channel_id=1, source_target_pairs={{8,0},{16,8},{24,16},{0,24},{9,1},{17,9},{25,17},{1,25},{10,2},{18... | collective-permute-start | bytes 24584 | tf_op jit(solution)/shard_map/ppermute | solution.py:18
  21.7 4.6 collective-permute-start.3
  39.2 3.1 fusion.131
  42.4 2.0 copy.77
  44.4 2.1 copy.76
  46.5 2.1 copy.75
  50.6 2.1 copy.73
  52.7 2.0 copy.72
  54.7 2.1 copy.71
  56.8 2.1 copy.70
  58.8 2.1 copy.69
  67.5 84.9 %all-gather.2.cloned.1.call-done = bf16[16,16,16,128]{3,2,1,0:T(8,128)(2,1)} async-done(((bf16[1,16,16,128]{3,2,1,0:T(8,128)(2,1)}), bf16[16,16,16,128]{3,2,1,0:T(8,128)(2,1)}) %all-gather.2.cloned.1.call-update) | async-done | bytes 1048592 | tf_op jit(solution)/shard_map/all_gather | solution.py:72
  154.6 6.5 %collective-permute-start.4 = (bf16[16,2,128]{2,0,1:T(8,128)(2,1)S(1)}, bf16[16,2,128]{2,0,1:T(8,128)(2,1)S(1)}, u32[]{:S(2)}, u32[]{:S(2)}) collective-permute-start(bf16[16,2,128]{2,0,1:T(8,128)(2,1)S(1)} %get-tuple-element.56), channel_id=1, source_target_pairs={{0,8},{8,16},{16,24},{24,0},{1,9},{9,17},{17,25},{25,1},{2,10},{10... | collective-permute-start | bytes 24584 | tf_op jit(solution)/shard_map/ppermute | solution.py:16
  166.1 3.1 collective-permute-start.6
  169.3 3.4 collective-permute-start.7
  187.4 2.4 reshape.190
  189.7 2.9 copy.90
  192.6 2.7 select_convert_fusion
  195.7 2.4 fusion.130
  200.9 2.1 copy.99
  203.0 2.1 copy.98
  205.0 2.1 copy.97
  213.3 258.9 %all-reduce.3.cloned.1.call-done = (f32[9,128,16]{1,2,0:T(8,128)}, f32[9,16,128]{2,1,0:T(8,128)}) async-done(((f32[9,128,16]{1,2,0:T(8,128)}, f32[9,16,128]{2,1,0:T(8,128)}), (f32[9,128,16]{1,2,0:T(8,128)}, f32[9,16,128]{2,1,0:T(8,128)})) %all-reduce.3.cloned.1.call-update) | async-done | bytes 147472 | tf_op jit(solution)/shard_map/psum | solution.py:102
  (193 shorter events, 59.2 us)
Async XLA Ops:
  7.2 145.2 %all-gather.2.cloned.1.call-start = ((), (), s32[]{:S(2)}) async-start(), calls=%async_computation | async-start | bytes 1114112 | tf_op jit(solution)/shard_map/all_gather | solution.py:72
  8.1 10.7 %collective-permute-start = (bf16[16,2,128]{2,0,1:T(8,128)(2,1)S(1)}, bf16[16,2,128]{2,0,1:T(8,128)(2,1)S(1)}, u32[]{:S(2)}, u32[]{:S(2)}) collective-permute-start(bf16[16,2,128]{2,0,1:T(8,128)(2,1)S(1)} %get-tuple-element.58), channel_id=1, source_target_pairs={{0,8},{8,16},{16,24},{24,0},{1,9},{9,17},{17,25},{25,1},{2,10},{10... | collective-permute-start | bytes 24584 | tf_op jit(solution)/shard_map/ppermute | solution.py:16
  12.6 7.0 %collective-permute-start.1 = (bf16[16,2,128]{2,0,1:T(8,128)(2,1)S(1)}, bf16[16,2,128]{2,0,1:T(8,128)(2,1)S(1)}, u32[]{:S(2)}, u32[]{:S(2)}) collective-permute-start(bf16[16,2,128]{2,0,1:T(8,128)(2,1)S(1)} %get-tuple-element.59), channel_id=1, source_target_pairs={{8,0},{16,8},{24,16},{0,24},{9,1},{17,9},{25,17},{1,25},{10,2},{18... | collective-permute-start | bytes 24584 | tf_op jit(solution)/shard_map/ppermute | solution.py:18
  19.7 6.6 %collective-permute-start.2 = (bf16[16,20,2]{2,0,1:T(8,128)(2,1)S(1)}, bf16[16,20,2]{2,0,1:T(8,128)(2,1)S(1)}, u32[]{:S(2)}, u32[]{:S(2)}) collective-permute-start(bf16[16,20,2]{2,0,1:T(8,128)(2,1)S(1)} %get-tuple-element.54), channel_id=1, source_target_pairs={{0,1},{1,2},{2,3},{3,4},{4,5},{5,6},{6,7},{7,0},{8,9},{9,10},{10,1... | collective-permute-start | bytes 3848 | tf_op jit(solution)/shard_map/ppermute | solution.py:16
  21.7 6.0 %collective-permute-start.3 = (bf16[16,20,2]{2,0,1:T(8,128)(2,1)S(1)}, bf16[16,20,2]{2,0,1:T(8,128)(2,1)S(1)}, u32[]{:S(2)}, u32[]{:S(2)}) collective-permute-start(bf16[16,20,2]{2,0,1:T(8,128)(2,1)S(1)} %get-tuple-element.55), channel_id=1, source_target_pairs={{1,0},{2,1},{3,2},{4,3},{5,4},{6,5},{7,6},{0,7},{9,8},{10,9},{11,1... | collective-permute-start | bytes 3848 | tf_op jit(solution)/shard_map/ppermute | solution.py:18
  36.5 1.9 copy-start.28
  60.9 2.7 copy-start.14
  60.9 2.8 copy-start.21
  60.9 3.0 copy-start.13
  62.3 1.9 copy-start.12
  64.4 1.2 copy-start.6
  65.0 1.5 copy-start.17
  67.3 404.9 %all-reduce.3.cloned.1.call-start = ((), (), s32[]{:S(2)}) async-start(), calls=%async_computation.1 | async-start | bytes 294912 | tf_op jit(solution)/shard_map/psum | solution.py:102
  152.4 1.8 copy-start.16
  152.4 1.8 copy-start.18
  152.4 1.8 copy-start.27
  154.3 20.2 %copy-start.2 = (bf16[16,16,128]{2,0,1:T(8,128)(2,1)}, bf16[16,16,128]{2,0,1:T(8,128)(2,1)S(1)}, u32[]{:S(2)}) copy-start(bf16[16,16,128]{2,0,1:T(8,128)(2,1)S(1)} %fusion.25) | copy-start | bytes 196612
  154.6 10.6 %collective-permute-start.4 = (bf16[16,2,128]{2,0,1:T(8,128)(2,1)S(1)}, bf16[16,2,128]{2,0,1:T(8,128)(2,1)S(1)}, u32[]{:S(2)}, u32[]{:S(2)}) collective-permute-start(bf16[16,2,128]{2,0,1:T(8,128)(2,1)S(1)} %get-tuple-element.56), channel_id=1, source_target_pairs={{0,8},{8,16},{16,24},{24,0},{1,9},{9,17},{17,25},{25,1},{2,10},{10... | collective-permute-start | bytes 24584 | tf_op jit(solution)/shard_map/ppermute | solution.py:16
  161.1 5.0 %collective-permute-start.5 = (bf16[16,2,128]{2,0,1:T(8,128)(2,1)S(1)}, bf16[16,2,128]{2,0,1:T(8,128)(2,1)S(1)}, u32[]{:S(2)}, u32[]{:S(2)}) collective-permute-start(bf16[16,2,128]{2,0,1:T(8,128)(2,1)S(1)} %get-tuple-element.57), channel_id=1, source_target_pairs={{8,0},{16,8},{24,16},{0,24},{9,1},{17,9},{25,17},{1,25},{10,2},{18... | collective-permute-start | bytes 24584 | tf_op jit(solution)/shard_map/ppermute | solution.py:18
  166.1 6.8 %collective-permute-start.6 = (bf16[16,20,2]{2,0,1:T(8,128)(2,1)S(1)}, bf16[16,20,2]{2,0,1:T(8,128)(2,1)S(1)}, u32[]{:S(2)}, u32[]{:S(2)}) collective-permute-start(bf16[16,20,2]{2,0,1:T(8,128)(2,1)S(1)} %get-tuple-element.52), channel_id=1, source_target_pairs={{0,1},{1,2},{2,3},{3,4},{4,5},{5,6},{6,7},{7,0},{8,9},{9,10},{10,1... | collective-permute-start | bytes 3848 | tf_op jit(solution)/shard_map/ppermute | solution.py:16
  169.3 5.2 %collective-permute-start.7 = (bf16[16,20,2]{2,0,1:T(8,128)(2,1)S(1)}, bf16[16,20,2]{2,0,1:T(8,128)(2,1)S(1)}, u32[]{:S(2)}, u32[]{:S(2)}) collective-permute-start(bf16[16,20,2]{2,0,1:T(8,128)(2,1)S(1)} %get-tuple-element.53), channel_id=1, source_target_pairs={{1,0},{2,1},{3,2},{4,3},{5,4},{6,5},{7,6},{0,7},{9,8},{10,9},{11,1... | collective-permute-start | bytes 3848 | tf_op jit(solution)/shard_map/ppermute | solution.py:18
  173.0 1.5 copy-start.25
  192.6 2.7 copy-start.1
  200.9 6.2 %copy-start.26 = (f32[9,128,16]{1,2,0:T(8,128)}, f32[9,128,16]{1,2,0:T(8,128)S(1)}, u32[]{:S(2)}) copy-start(f32[9,128,16]{1,2,0:T(8,128)S(1)} %fusion.12) | copy-start | bytes 221188
  (15 other events, 14.6 us)
Sparse Core Ops, SparseCore 0:
  67.4 84.9 all-gather.1
  210.2 261.9 all-reduce.2
where the time goes:
time: 483 us; the launch traced here: 482 us
  waiting for transfers between devices  348 us (72%)
  local copies, waits for them, and re-layouts  54.6 us (11%)
  starting transfers between devices  32.4 us (7%)
  matrix products  22.6 us (5%)
  between operations  14.6 us (3%)
  other arithmetic  9.47 us (2%)
    psum x1, waiting for transfers between devices, shards(): lax.psum((jnp.stack(in_terms), jnp.stack(out_terms)), ('member', 'lat', '...  259 us
    all_gather x1, waiting for transfers between devices, shards(): lax.all_gather(prediction[None], 'member', axis=0, tiled=True)  84.9 us
    slice x40, local copies, waits for them, and re-layouts, stencil_at(): padded[:, start_row:start_row + row_count, start_col:start_col + col_count]  36.7 us
    dot_general x36, matrix products, stencil_at(): term = jnp.dot(matrix, window, preferred_element_type=jnp.float32)  16.7 us
    ppermute x4, starting transfers between devices, extended(): lax.ppermute(head, axis, [((i + 1) % count, i) for i in range(count)])  16.1 us
    ppermute x4, starting transfers between devices, extended(): lax.ppermute(tail, axis, [(i, (i + 1) % count) for i in range(count)])  16 us
  transfers between devices with their start and end apart: 10, of which 6 were waited for; matrix products, arithmetic and copies ran while one was open for 1% of the time, Pallas kernels for 0%

commit v1 on v0

v1 whole, which is shorter than its diff:
```python
import functools
import math

import jax
import jax.numpy as jnp
from jax import lax
from jax.experimental import pallas as pl
from jax.experimental.pallas import tpu as pltpu
from jax.sharding import PartitionSpec as P

MESH = pl.DeviceIdType.MESH
F32 = jnp.float32
BF16 = jnp.bfloat16

LEV = 16
C = 128
ROWS = 16
COLS = 128
HALO = 4
PITCH = COLS + 2 * HALO
FLAT = 26 * 128
LEAD = 128
OFFSETS = [(di, dj) for di in (-1, 0, 1) for dj in (-1, 0, 1)]
SHIFTS = [di * PITCH + dj for di, dj in OFFSETS]
PRED_FIRST = 2
PRED_TILES = 22
TAPS = 9 * LEV
PART = TAPS // 8


def ring_order(count):
    return sorted(range(count), key=lambda d: (-min(d, count - d), d))


def kernel(
    sizes,
    x_hbm,
    t_hbm,
    w_in_hbm,
    bias_ref,
    w_out_hbm,
    field_hbm,
    gin_ref,
    gout_ref,
    x16,
    t16,
    win16,
    wout16,
    rows32,
    xf,
    w_in,
    w_in_t,
    w_out_t,
    bias,
    side_send,
    band_send,
    side_recv,
    band_recv,
    xc,
    pre,
    act,
    act_own,
    taps,
    pred_send,
    pred_recv,
    target_tiles,
    grad_send,
    grad_recv,
    gp,
    gc,
    gh,
    field,
    part_sum,
    part_recv,
    lon_recv,
    mem_recv,
    all_recv,
    load_sem,
    send_sem,
    recv_sem,
):
    members, lats, lons = sizes
    zs = members // 2
    quads = 2 * lats
    share = -(-PRED_TILES // members)
    chunk = -(-PART // quads)
    me_m = lax.axis_index("member")
    me_a = lax.axis_index("lat")
    me_o = lax.axis_index("lon")
    me_z = me_m // 2
    me_h = me_m % 2
    me_q = me_h * lats + me_a

    loads = [
        pltpu.make_async_copy(src, dst, load_sem.at[i])
        for i, (src, dst) in enumerate(
            ((x_hbm.at[0], x16), (t_hbm, t16), (w_in_hbm, win16), (w_out_hbm, wout16))
        )
    ]
    for load in loads:
        load.start()

    def at(dm_z, dm_h, da, do):
        return (
            ((me_z + dm_z) % zs) * 2 + (me_h + dm_h) % 2,
            (me_a + da + lats) % lats,
            (me_o + do + lons) % lons,
        )

    halo = [(da, do) for da, do in ((-1, -1), (-1, 1), (1, -1), (1, 1), (0, -1), (0, 1), (-1, 0), (1, 0))]
    group_m = [(dz, h) for dz in ring_order(zs) for h in (1, 0) if dz or h]
    group_q = [(h, da) for h in (1, 0) for da in ring_order(lats) if h or da]
    group_o = [d for d in ring_order(lons) if d]
    group_z = [d for d in ring_order(zs) if d]

    barrier = pltpu.get_barrier_semaphore()
    greet = [at(dz, h, 0, 0) for dz, h in group_m]
    greet += [at(0, 0, 0, d) for d in group_o]
    greet += [at(0, h, da, 0) for h, da in group_q]
    greet += [at(0, 0, da, do) for da, do in halo]
    for device in greet:
        pl.semaphore_signal(barrier, inc=1, device_id=device, device_id_type=MESH)

    loads[0].wait()
    loads[1].wait()
    rows32[0:LEV] = x16[...].astype(F32)
    rows32[LEV:] = t16[...].astype(F32)
    for r in range(ROWS):
        start = LEAD + PITCH * (r + HALO) + HALO
        xf[:, start : start + COLS] = rows32[:, r, :]

    def place(first, height, width):
        lane = lax.broadcasted_iota(jnp.int32, (height, width), 1).astype(F32) + float(first)
        row = jnp.floor((lane + 0.5) * (1.0 / PITCH))
        return row, lane - PITCH * row

    left_edge = jnp.zeros((2 * LEV, 128), F32)
    right_edge = jnp.zeros((2 * LEV, 128), F32)
    for t in range(4, 22):
        row, col = place(t * 128, 2 * LEV, 128)
        here = (row >= HALO) & (row < HALO + ROWS)
        tile = xf[:, LEAD + t * 128 : LEAD + t * 128 + 128]
        left_edge += jnp.where(here & (col >= HALO) & (col < 2 * HALO), tile, 0.0)
        right_edge += jnp.where(here & (col >= COLS) & (col < COLS + HALO), tile, 0.0)
    side_send[0] = right_edge.astype(BF16)
    side_send[1] = left_edge.astype(BF16)
    band_send[0] = xf[:, LEAD + 17 * 128 : LEAD + 22 * 128].astype(BF16)
    band_send[1] = xf[:, LEAD + 4 * 128 : LEAD + 9 * 128].astype(BF16)

    loads[2].wait()
    loads[3].wait()
    wide = jnp.concatenate([win16[k].astype(F32) for k in range(9)], axis=1)
    w_in[...] = wide.astype(BF16)
    w_in_t[...] = wide.T.astype(BF16)
    w_out = wout16[...].reshape(TAPS, C)
    w_out_t[...] = w_out.astype(F32).T.astype(BF16)
    bias[...] = jnp.broadcast_to(bias_ref[...], (C, C)).T
    taps[:, 0:128] = jnp.zeros((TAPS, 128), F32)
    taps[:, FLAT - 128 : FLAT] = jnp.zeros((TAPS, 128), F32)
    xf[:, 0:LEAD] = jnp.zeros((2 * LEV, LEAD), F32)
    xf[:, LEAD + FLAT :] = jnp.zeros((2 * LEV, 128), F32)
    gp[...] = jnp.zeros_like(gp)
    target_tiles[...] = jnp.zeros_like(target_tiles)
    pred_send[...] = jnp.zeros_like(pred_send)

    pl.semaphore_wait(barrier, len(greet))

    sends = []

    def send(src, dst, phase, device):
        copy = pltpu.make_async_remote_copy(
            src_ref=src,
            dst_ref=dst,
            send_sem=send_sem.at[phase],
            recv_sem=recv_sem.at[phase],
            device_id=device,
            device_id_type=MESH,
        )
        copy.start()

    def wait_recv(ref, phase):
        pltpu.make_async_remote_copy(
            src_ref=ref,
            dst_ref=ref,
            send_sem=send_sem.at[phase],
            recv_sem=recv_sem.at[phase],
            device_id=(me_m, me_a, (me_o + 1) % lons),
            device_id_type=MESH,
        ).wait_recv()

    def wait_send(ref, phase):
        pltpu.make_async_remote_copy(
            src_ref=ref,
            dst_ref=ref,
            send_sem=send_sem.at[phase],
            recv_sem=recv_sem.at[phase],
            device_id=(me_m, me_a, (me_o + 1) % lons),
            device_id_type=MESH,
        ).wait_send()

    for da in (-1, 1, 0):
        send(side_send.at[0], side_recv.at[0, 1 - da], 0, at(0, 0, da, 1))
        send(side_send.at[1], side_recv.at[1, 1 - da], 0, at(0, 0, da, -1))
    send(band_send.at[0], band_recv.at[0], 1, at(0, 0, 1, 0))
    send(band_send.at[1], band_recv.at[1], 1, at(0, 0, -1, 0))

    wait_recv(side_recv, 0)
    wait_recv(band_recv, 1)

    row_low = jnp.where(me_a == 0, HALO, 0).astype(F32)
    row_high = jnp.where(me_a == lats - 1, HALO + ROWS, ROWS + 2 * HALO).astype(F32)
    sides = [[side_recv[i, j].astype(F32) for j in range(3)] for i in range(2)]
    for t in range(26):
        row, col = place(t * 128, 2 * LEV, 128)
        tile = xf[:, LEAD + t * 128 : LEAD + t * 128 + 128]
        left, right = sides[0][1], sides[1][1]
        if t < 5:
            above = row < HALO
            tile = jnp.where(above, band_recv[0, :, t * 128 : t * 128 + 128].astype(F32), tile)
            left = jnp.where(above, sides[0][0], left)
            right = jnp.where(above, sides[1][0], right)
        if t >= 21:
            below = row >= HALO + ROWS
            tile = jnp.where(below, band_recv[1, :, (t - 21) * 128 : (t - 20) * 128].astype(F32), tile)
            left = jnp.where(below, sides[0][2], left)
            right = jnp.where(below, sides[1][2], right)
        tile = jnp.where(col < HALO, left, tile)
        tile = jnp.where(col >= HALO + COLS, right, tile)
        if t < 5 or t >= 21:
            tile = jnp.where((row >= row_low) & (row < row_high), tile, 0.0)
        xf[:, LEAD + t * 128 : LEAD + t * 128 + 128] = tile
        if PRED_FIRST <= t < PRED_FIRST + PRED_TILES:
            target_tiles[t - PRED_FIRST] = tile[LEV:]

    for k, shift in enumerate(SHIFTS):
        xc[k * LEV : (k + 1) * LEV, 128:3200] = xf[0:LEV, LEAD + 128 + shift : LEAD + 3200 + shift].astype(BF16)

    def forward(i, carry):
        start = pl.multiple_of(128 + i * 256, 128)
        lanes = pl.ds(start, 256)
        hidden = jnp.dot(w_in[...], xc[:, lanes], preferred_element_type=F32)
        hidden += jnp.concatenate([bias[...], bias[...]], axis=1)
        pre[:, lanes] = hidden
        lane = lax.broadcasted_iota(jnp.int32, (C, 256), 1) + start
        inside = (lane >= low_lane) & (lane < high_lane)
        value = jnp.where(inside, hidden * jax.nn.sigmoid(hidden), 0.0).astype(BF16)
        act[:, lanes] = value
        taps[:, lanes] = jnp.dot(
            wout16[...].reshape(TAPS, C), value, preferred_element_type=F32
        )
        return carry

    low_lane = jnp.where(me_a == 0, HALO * PITCH, 0)
    high_lane = jnp.where(me_a == lats - 1, (HALO + ROWS) * PITCH, FLAT)
    lax.fori_loop(0, 12, forward, 0)

    for t in range(0, PRED_TILES, 2):
        first = (PRED_FIRST + t) * 128
        total = xf[0:LEV, LEAD + first : LEAD + first + 256]
        for k, shift in enumerate(SHIFTS):
            total += taps[k * LEV : (k + 1) * LEV, first + shift : first + shift + 256]
        for u in (t, t + 1):
            pred_send[u % members, u // members] = total[:, (u - t) * 128 : (u - t + 1) * 128].astype(BF16)

    for dz, h in group_m:
        device = at(dz, h, 0, 0)
        send(pred_send.at[device[0]], pred_recv.at[me_m], 2, device)
    pred_recv[me_m] = pred_send[me_m]

    def own_slopes(i, carry):
        start = pl.multiple_of(384 + i * 256, 128)
        lanes = pl.ds(start, 256)
        hidden = pre[:, lanes]
        gate = jax.nn.sigmoid(hidden)
        pre[:, lanes] = gate * (1.0 + hidden * (1.0 - gate))
        row, col = place(0, C, 256)
        lane = lax.broadcasted_iota(jnp.int32, (C, 256), 1).astype(F32) + start.astype(F32)
        row = jnp.floor((lane + 0.5) * (1.0 / PITCH))
        col = lane - PITCH * row
        own = (row >= HALO) & (row < HALO + ROWS) & (col >= HALO) & (col < HALO + COLS)
        act_own[:, lanes] = jnp.where(own, act[:, lanes].astype(F32), 0.0).astype(BF16)
        return carry

    lax.fori_loop(0, 10, own_slopes, 0)
    wait_recv(pred_recv.at[pl.ds(0, members - 1)], 2)

    coupling = (1.0 - 0.05 / members) / (members - 1)

    def slope(d):
        return d * lax.rsqrt(d * d + 0.25)

    for u in range(share):
        everyone = pred_recv[:, u].astype(F32)
        wanted = target_tiles[me_m + u * members]
        for half in range(2):
            own = everyone[:, half * 8 : half * 8 + 8]
            spread = jnp.zeros_like(own)
            for d in range(1, members // 2 + 1):
                term = slope(own - jnp.concatenate([own[d:], own[:d]], axis=0))
                spread += term
                if 2 * d != members:
                    spread -= jnp.concatenate([term[members - d :], term[: members - d]], axis=0)
            value = slope(own - wanted[None, half * 8 : half * 8 + 8]) - coupling * spread
            field[:, half * 8 : half * 8 + 8, :] = value
        grad_send[:, u] = field[...].astype(BF16)

    for dz, h in group_m:
        device = at(dz, h, 0, 0)
        send(grad_send.at[device[0]], grad_recv.at[me_m], 3, device)
    grad_recv[me_m] = grad_send[me_m]
    wait_recv(grad_recv.at[pl.ds(0, members - 1)], 3)

    for u in range(PRED_TILES):
        t = PRED_FIRST + u
        row, col = place(t * 128, LEV, 128)
        inside = (row >= row_low) & (row < row_high) & (col >= HALO - 2) & (col < HALO + COLS + 2)
        tile = grad_recv[u % members, u // members].astype(F32)
        gp[:, t * 128 : t * 128 + 128] = jnp.where(inside, tile, 0.0)
    for k, shift in enumerate(SHIFTS):
        gc[k * LEV : (k + 1) * LEV, 384:2944] = gp[:, 384 - shift : 2944 - shift].astype(BF16)

    contract_lanes = (((1,), (1,)), ((), ()))
    out_part = lax.dot_general(
        gc[:, 512:2816], act_own[:, 512:2816], contract_lanes, preferred_element_type=F32
    )
    part_sum[0, 0:PART] = out_part.reshape(PART, 8, C)
    part_sum[0, PART:] = jnp.zeros((quads * chunk - PART, 8, C), F32)
    for h, da in group_q:
        device = at(0, h, da, 0)
        slot = (device[0] % 2) * lats + device[1]
        send(part_sum.at[0, pl.ds(slot * chunk, chunk)], part_recv.at[0, me_q], 4, device)

    def backward(i, carry):
        start = pl.multiple_of(384 + i * 256, 128)
        lanes = pl.ds(start, 256)
        value = jnp.dot(w_out_t[...], gc[:, lanes], preferred_element_type=F32) * pre[:, lanes]
        lane = lax.broadcasted_iota(jnp.int32, (C, 256), 1)
        inside = (lane + start >= low_lane) & (lane + start < high_lane)
        value = jnp.where(inside, value, 0.0)
        spread = lane.astype(F32) + start.astype(F32)
        row = jnp.floor((spread + 0.5) * (1.0 / PITCH))
        col = spread - PITCH * row
        own = (row >= HALO) & (row < HALO + ROWS) & (col >= HALO) & (col < HALO + COLS)
        gh[:, lanes] = jnp.where(own, value, 0.0).astype(BF16)
        taps[:, lanes] = jnp.dot(w_in_t[...], value.astype(BF16), preferred_element_type=F32)
        return carry

    lax.fori_loop(0, 10, backward, 0)
    in_part = lax.dot_general(
        xc[:, 512:2816], gh[:, 512:2816], contract_lanes, preferred_element_type=F32
    )
    part_sum[1, 0:PART] = in_part.reshape(PART, 8, C)
    part_sum[1, PART:] = jnp.zeros((quads * chunk - PART, 8, C), F32)
    for h, da in group_q:
        device = at(0, h, da, 0)
        slot = (device[0] % 2) * lats + device[1]
        send(part_sum.at[1, pl.ds(slot * chunk, chunk)], part_recv.at[1, me_q], 5, device)
    for p in range(2):
        part_recv[p, me_q] = part_sum[p, pl.ds(me_q * chunk, chunk)]

    for r in range(ROWS):
        start = PITCH * (r + HALO) + HALO
        total = gp[:, start : start + COLS]
        for k, shift in enumerate(SHIFTS):
            total += taps[k * LEV : (k + 1) * LEV, start - shift : start - shift + COLS]
        field[:, r, :] = total
    store = pltpu.make_async_copy(field, field_hbm.at[0], load_sem.at[0])
    store.start()

    wait_recv(part_recv.at[0, pl.ds(0, quads - 1)], 4)
    wait_recv(part_recv.at[1, pl.ds(0, quads - 1)], 5)
    for p in range(2):
        total = part_recv[p, 0]
        for q in range(1, quads):
            total += part_recv[p, q]
        lon_recv[me_o, pl.ds(p * chunk, chunk)] = total
    for d in group_o:
        send(lon_recv.at[me_o], lon_recv.at[me_o], 6, at(0, 0, 0, d))
    wait_recv(lon_recv.at[pl.ds(0, lons - 1)], 6)
    total = lon_recv[0]
    for i in range(1, lons):
        total += lon_recv[i]
    mem_recv[me_z] = total
    for d in group_z:
        send(mem_recv.at[me_z], mem_recv.at[me_z], 7, at(d, 0, 0, 0))
    wait_recv(mem_recv.at[pl.ds(0, zs - 1)], 7)
    total = mem_recv[0]
    for i in range(1, zs):
        total += mem_recv[i]
    all_recv[me_q] = total * (1.0 / math.sqrt(members * lats * lons * ROWS * COLS))
    for h, da in group_q:
        send(all_recv.at[me_q], all_recv.at[me_q], 8, at(0, h, da, 0))
    wait_recv(all_recv.at[pl.ds(0, quads - 1)], 8)

    for t in range(PART):
        k, half = t // 2, t % 2
        gout_ref[k, half * 8 : half * 8 + 8, :] = all_recv[t // chunk, t % chunk]
    for k in range(9):
        pair = [all_recv[t // chunk, chunk + t % chunk] for t in (2 * k, 2 * k + 1)]
        gin_ref[k] = jnp.concatenate(pair, axis=0).T

    store.wait()
    wait_send(side_recv, 0)
    wait_send(band_recv, 1)
    wait_send(pred_recv.at[pl.ds(0, members - 1)], 2)
    wait_send(grad_recv.at[pl.ds(0, members - 1)], 3)
    wait_send(part_recv.at[0, pl.ds(0, quads - 1)], 4)
    wait_send(part_recv.at[1, pl.ds(0, quads - 1)], 5)
    wait_send(lon_recv.at[pl.ds(0, lons - 1)], 6)
    wait_send(mem_recv.at[pl.ds(0, zs - 1)], 7)
    wait_send(all_recv.at[pl.ds(0, quads - 1)], 8)


def shards(sizes, inputs, target, conv_in, bias_in, conv_out):
    members, lats, lons = sizes
    quads = 2 * lats
    share = -(-PRED_TILES // members)
    chunk = -(-PART // quads)
    wide = FLAT + LEAD + 128
    return pl.pallas_call(
        functools.partial(kernel, sizes),
        out_shape=(
            jax.ShapeDtypeStruct((1, LEV, ROWS, COLS), F32),
            jax.ShapeDtypeStruct((9, C, LEV), F32),
            jax.ShapeDtypeStruct((9, LEV, C), F32),
        ),
        in_specs=[
            pl.BlockSpec(memory_space=pl.ANY),
            pl.BlockSpec(memory_space=pl.ANY),
            pl.BlockSpec(memory_space=pl.ANY),
            pl.BlockSpec(memory_space=pltpu.VMEM),
            pl.BlockSpec(memory_space=pl.ANY),
        ],
        out_specs=(
            pl.BlockSpec(memory_space=pl.ANY),
            pl.BlockSpec(memory_space=pltpu.VMEM),
            pl.BlockSpec(memory_space=pltpu.VMEM),
        ),
        scratch_shapes=[
            pltpu.VMEM((LEV, ROWS, COLS), BF16),
            pltpu.VMEM((LEV, ROWS, COLS), BF16),
            pltpu.VMEM((9, C, LEV), BF16),
            pltpu.VMEM((9, LEV, C), BF16),
            pltpu.VMEM((2 * LEV, ROWS, COLS), F32),
            pltpu.VMEM((2 * LEV, wide), F32),
            pltpu.VMEM((C, TAPS), BF16),
            pltpu.VMEM((TAPS, C), BF16),
            pltpu.VMEM((C, TAPS), BF16),
            pltpu.VMEM((C, C), F32),
            pltpu.VMEM((2, 2 * LEV, 128), BF16),
            pltpu.VMEM((2, 2 * LEV, 640), BF16),
            pltpu.VMEM((2, 3, 2 * LEV, 128), BF16),
            pltpu.VMEM((2, 2 * LEV, 640), BF16),
            pltpu.VMEM((TAPS, FLAT), BF16),
            pltpu.VMEM((C, FLAT), F32),
            pltpu.VMEM((C, FLAT), BF16),
            pltpu.VMEM((C, FLAT), BF16),
            pltpu.VMEM((TAPS, FLAT), F32),
            pltpu.VMEM((members, share, LEV, 128), BF16),
            pltpu.VMEM((members, share, LEV, 128), BF16),
            pltpu.VMEM((members * share, LEV, 128), F32),
            pltpu.VMEM((members, share, LEV, 128), BF16),
            pltpu.VMEM((members, share, LEV, 128), BF16),
            pltpu.VMEM((LEV, FLAT), F32),
            pltpu.VMEM((TAPS, FLAT), BF16),
            pltpu.VMEM((C, FLAT), BF16),
            pltpu.VMEM((LEV, ROWS, COLS), F32),
            pltpu.VMEM((2, quads * chunk, 8, C), F32),
            pltpu.VMEM((2, quads, chunk, 8, C), F32),
            pltpu.VMEM((lons, 2 * chunk, 8, C), F32),
            pltpu.VMEM((members // 2, 2 * chunk, 8, C), F32),
            pltpu.VMEM((quads, 2 * chunk, 8, C), F32),
            pltpu.SemaphoreType.DMA((4,)),
            pltpu.SemaphoreType.DMA((9,)),
            pltpu.SemaphoreType.DMA((9,)),
        ],
        compiler_params=pltpu.CompilerParams(
            collective_id=0, has_side_effects=True, vmem_limit_bytes=40 * 1024 * 1024
        ),
        name="downscaling_step",
    )(inputs, target, conv_in, bias_in.reshape(1, C), conv_out)


def solution(mesh):
    sizes = tuple(mesh.shape[axis] for axis in ("member", "lat", "lon"))
    in_specs = (P("member", None, "lat", "lon"), P(None, "lat", "lon"), P(), P(), P())
    out_specs = (P("member", None, "lat", "lon"), P(), P())
    return jax.shard_map(
        functools.partial(shards, sizes),
        mesh=mesh,
        in_specs=in_specs,
        out_specs=out_specs,
        check_vma=False,
    )
```

time: 483 us -> 66.7 us (0.14)
  waiting for transfers between devices: 348 us -> 0 us
  Pallas kernels: 0 us -> 62.7 us
  local copies, waits for them, and re-layouts: 54.6 us -> 3.18 us
  starting transfers between devices: 32.4 us -> 0 us
  matrix products: 22.6 us -> 0 us
  between operations: 14.6 us -> 0.7 us
  other arithmetic: 9.47 us -> 0 us
    psum x1 -> x0, waiting for transfers between devices: 259 us -> none  [shards(): lax.psum((jnp.stack(in_terms), jnp.stack(out_terms)), ('member', 'lat', '...]
    all_gather x1 -> x0, waiting for transfers between devices: 84.9 us -> none  [shards(): lax.all_gather(prediction[None], 'member', axis=0, tiled=True)]
    pallas_call x0 -> x1, Pallas kernels: none -> 62.7 us  [shards(): pl.pallas_call(functools.partial(kernel, sizes), out_shape=(jax.ShapeDtyp...]
    slice x45 -> x0, local copies, waits for them, and re-layouts: 37 us -> none  [the longest x40 36.7 us: stencil_at(): padded[:, start_row:start_row + row_count, start_col:start_col + col_count]]
    ppermute x8 -> x0, starting transfers between devices: 32.1 us -> none  [the longest x4 16.1 us: extended(): lax.ppermute(head, axis, [((i + 1) % count, i) for i in range(count)])]
    dot_general x54 -> x0, matrix products: 22.6 us -> none  [the longest x36 16.7 us: stencil_at(): term = jnp.dot(matrix, window, preferred_element_type=jnp.float32)]
    reshape x22 -> x0, local copies, waits for them, and re-layouts: 13 us -> none  [the longest x4 8.25 us: stencil_at(): return running.reshape(-1, row_count, col_count)]
  transfers between devices with their start and end apart: 10 -> 0, of which waited for: 6 -> 0; matrix products, arithmetic and copies ran while one was open for 1% -> 0% of each run, Pallas kernels for 0% -> 0%
where the time goes in v1:
time: 66.7 us; the launch traced here: 66.6 us
  Pallas kernels  62.7 us (94%)
  local copies, waits for them, and re-layouts  3.18 us (5%)
  between operations  0.7 us (1%)
    pallas_call x1, Pallas kernels, shards(): pl.pallas_call(functools.partial(kernel, sizes), out_shape=(jax.ShapeDtyp...  62.7 us
    unnamed x11, local copies, waits for them, and re-layouts  2.34 us

profile of v1, /device:TPU:1, one launch (start us, length us, event | category | flops | bytes accessed | tf_op | source)
XLA Modules:
  0.0 66.6 jit_solution(3992379865562078942)
XLA Ops:
  0.6 0.0 copy-start
  0.6 0.0 copy-start.1
  0.7 0.0 copy-start.2
  0.7 0.0 copy-start.3
  0.7 1.0 %copy.8.w_in_hbm = bf16[9,128,16]{2,1,0:T(8,128)(2,1)S(1)} copy(bf16[9,128,16]{1,2,0:T(8,128)(2,1)} %param.7) | data formatting | bytes 73728 | tf_op args[2]
  1.7 0.0 copy-done
  1.7 0.0 copy-done.1
  1.7 0.0 copy-done.2
  1.7 0.0 copy-done.3
  1.7 62.7 %downscaling_step.1 = (f32[1,16,16,128]{3,2,1,0:T(8,128)S(1)}, f32[9,128,16]{2,1,0:T(8,128)S(1)}, f32[9,16,128]{2,1,0:T(8,128)S(1)}) custom-call(bf16[1,16,16,128]{3,2,1,0:T(8,128)(2,1)S(1)} %copy-done, bf16[16,16,128]{2,1,0:T(8,128)(2,1)S(1)} %copy-done.1, bf16[9,128,16]{2,1,0:T(8,128)(2,1)S(1)} %copy.8.w_in_hbm, f32[1,128]{1,0:T(1,128)S(1)} %bitcast.1, ...), custom_call_target="tpu_custom_call" | custom-call | tf_op jit(solution)/shard_map/downscaling_step/pallas_call | solution.py:420
  64.4 0.8 %copy.9 = f32[9,128,16]{1,2,0:T(8,128)} copy(f32[9,128,16]{2,1,0:T(8,128)S(1)} %get-tuple-element.4) | data formatting | bytes 147456 | tf_op jit(solution)/shard_map/downscaling_step/pallas_call | solution.py:420
  65.3 0.7 copy.12
  65.9 0.6 copy.13
Async XLA Ops:
  0.6 1.1 %copy-start = (bf16[1,16,16,128]{3,2,1,0:T(8,128)(2,1)S(1)}, bf16[1,16,16,128]{3,2,1,0:T(8,128)(2,1)}, u32[]{:S(2)}) copy-start(bf16[1,16,16,128]{3,2,1,0:T(8,128)(2,1)} %x_hbm.1) | copy-start | bytes 196612
  0.6 1.1 %copy-start.1 = (bf16[16,16,128]{2,1,0:T(8,128)(2,1)S(1)}, bf16[16,16,128]{2,1,0:T(8,128)(2,1)}, u32[]{:S(2)}) copy-start(bf16[16,16,128]{2,1,0:T(8,128)(2,1)} %t_hbm.1) | copy-start | bytes 196612
  0.7 1.1 %copy-start.2 = (bf16[9,16,128]{2,1,0:T(8,128)(2,1)S(1)}, bf16[9,16,128]{2,1,0:T(8,128)(2,1)}, u32[]{:S(2)}) copy-start(bf16[9,16,128]{2,1,0:T(8,128)(2,1)} %w_out_hbm.1) | copy-start | bytes 110596
  0.7 1.1 %copy-start.3 = (f32[128]{0:T(128)S(1)}, f32[128]{0:T(128)}, u32[]{:S(2)}) copy-start(f32[128]{0:T(128)} %param.8) | copy-start | bytes 1540

commit v2 on v1

--- a/solution.py
+++ b/solution.py
@@ -26,6 +26,7 @@
 PRED_TILES = 22
 TAPS = 9 * LEV
 PART = TAPS // 8
+VMEM_LIMIT = 40 * 1024 * 1024
 
 
 def ring_order(count):
@@ -39,19 +40,19 @@
     w_in_hbm,
     bias_ref,
     w_out_hbm,
-    field_hbm,
-    gin_ref,
-    gout_ref,
+    field,
+    sums_ref,
     x16,
     t16,
-    win16,
-    wout16,
+    w_in_t,
+    w_out,
+    bias16,
     rows32,
     xf,
     w_in,
-    w_in_t,
     w_out_t,
     bias,
+    masks,
     side_send,
     band_send,
     side_recv,
@@ -64,12 +65,14 @@
     pred_send,
     pred_recv,
     target_tiles,
+    grads,
     grad_send,
     grad_recv,
     gp,
     gc,
     gh,
-    field,
+    gh_own,
+    by_row,
     part_sum,
     part_recv,
     lon_recv,
@@ -94,7 +97,13 @@
     loads = [
         pltpu.make_async_copy(src, dst, load_sem.at[i])
         for i, (src, dst) in enumerate(
-            ((x_hbm.at[0], x16), (t_hbm, t16), (w_in_hbm, win16), (w_out_hbm, wout16))
+            (
+                (x_hbm.at[0], x16),
+                (t_hbm, t16),
+                (w_in_hbm, w_in_t),
+                (w_out_hbm, w_out),
+                (bias_ref, bias16),
+            )
         )
     ]
     for load in loads:
@@ -147,25 +156,7 @@
     band_send[0] = xf[:, LEAD + 17 * 128 : LEAD + 22 * 128].astype(BF16)
     band_send[1] = xf[:, LEAD + 4 * 128 : LEAD + 9 * 128].astype(BF16)
 
-    loads[2].wait()
-    loads[3].wait()
-    wide = jnp.concatenate([win16[k].astype(F32) for k in range(9)], axis=1)
-    w_in[...] = wide.astype(BF16)
-    w_in_t[...] = wide.T.astype(BF16)
-    w_out = wout16[...].reshape(TAPS, C)
-    w_out_t[...] = w_out.astype(F32).T.astype(BF16)
-    bias[...] = jnp.broadcast_to(bias_ref[...], (C, C)).T
-    taps[:, 0:128] = jnp.zeros((TAPS, 128), F32)
-    taps[:, FLAT - 128 : FLAT] = jnp.zeros((TAPS, 128), F32)
-    xf[:, 0:LEAD] = jnp.zeros((2 * LEV, LEAD), F32)
-    xf[:, LEAD + FLAT :] = jnp.zeros((2 * LEV, 128), F32)
-    gp[...] = jnp.zeros_like(gp)
-    target_tiles[...] = jnp.zeros_like(target_tiles)
-    pred_send[...] = jnp.zeros_like(pred_send)
-
     pl.semaphore_wait(barrier, len(greet))
-
-    sends = []
 
     def send(src, dst, phase, device):
         copy = pltpu.make_async_remote_copy(
@@ -204,11 +195,34 @@
     send(band_send.at[0], band_recv.at[0], 1, at(0, 0, 1, 0))
     send(band_send.at[1], band_recv.at[1], 1, at(0, 0, -1, 0))
 
+    for load in loads[2:]:
+        load.wait()
+    w_in[...] = w_in_t[...].astype(F32).T.astype(BF16)
+    w_out_t[...] = w_out[...].astype(F32).T.astype(BF16)
+    bias[...] = jnp.broadcast_to(bias16[...], (C, C)).T
+    taps[:, 0:128] = jnp.zeros((TAPS, 128), F32)
+    taps[:, FLAT - 128 : FLAT] = jnp.zeros((TAPS, 128), F32)
+    xf[:, 0:LEAD] = jnp.zeros((2 * LEV, LEAD), F32)
+    xf[:, LEAD + FLAT :] = jnp.zeros((2 * LEV, 128), F32)
+    gp[:, 0 : PRED_FIRST * 128] = jnp.zeros((LEV, PRED_FIRST * 128), F32)
+    gp[:, (PRED_FIRST + PRED_TILES) * 128 :] = jnp.zeros((LEV, PRED_FIRST * 128), F32)
+    spare = members * share - PRED_TILES
+    for u in range(PRED_TILES, PRED_TILES + spare):
+        target_tiles[u] = jnp.zeros((LEV, 128), F32)
+        pred_send[u % members, u // members] = jnp.zeros((LEV, 128), BF16)
+    for p in range(2):
+        part_sum[p, PART:] = jnp.zeros((quads * chunk - PART, 8, C), F32)
+    row_low = jnp.where(me_a == 0, HALO, 0).astype(F32)
+    row_high = jnp.where(me_a == lats - 1, HALO + ROWS, ROWS + 2 * HALO).astype(F32)
+    row, col = place(0, 8, FLAT)
+    masks[0] = jnp.where((row >= row_low) & (row < row_high), 1.0, 0.0)
+    masks[1] = jnp.where(
+        (row >= HALO) & (row < HALO + ROWS) & (col >= HALO) & (col < HALO + COLS), 1.0, 0.0
+    )
+
     wait_recv(side_recv, 0)
     wait_recv(band_recv, 1)
 
-    row_low = jnp.where(me_a == 0, HALO, 0).astype(F32)
-    row_high = jnp.where(me_a == lats - 1, HALO + ROWS, ROWS + 2 * HALO).astype(F32)
     sides = [[side_recv[i, j].astype(F32) for j in range(3)] for i in range(2)]
     for t in range(26):
         row, col = place(t * 128, 2 * LEV, 128)
@@ -235,24 +249,15 @@
     for k, shift in enumerate(SHIFTS):
         xc[k * LEV : (k + 1) * LEV, 128:3200] = xf[0:LEV, LEAD + 128 + shift : LEAD + 3200 + shift].astype(BF16)
 
-    def forward(i, carry):
-        start = pl.multiple_of(128 + i * 256, 128)
-        lanes = pl.ds(start, 256)
-        hidden = jnp.dot(w_in[...], xc[:, lanes], preferred_element_type=F32)
-        hidden += jnp.concatenate([bias[...], bias[...]], axis=1)
-        pre[:, lanes] = hidden
-        lane = lax.broadcasted_iota(jnp.int32, (C, 256), 1) + start
-        inside = (lane >= low_lane) & (lane < high_lane)
-        value = jnp.where(inside, hidden * jax.nn.sigmoid(hidden), 0.0).astype(BF16)
-        act[:, lanes] = value
-        taps[:, lanes] = jnp.dot(
-            wout16[...].reshape(TAPS, C), value, preferred_element_type=F32
-        )
-        return carry
-
-    low_lane = jnp.where(me_a == 0, HALO * PITCH, 0)
-    high_lane = jnp.where(me_a == lats - 1, (HALO + ROWS) * PITCH, FLAT)
-    lax.fori_loop(0, 12, forward, 0)
+    def mask(which, first, last):
+        return masks[which, 0:1, first:last] > 0.5
+
+    hidden = jnp.dot(w_in[...], xc[:, 128:3200], preferred_element_type=F32)
+    hidden += jnp.concatenate([bias[...]] * 24, axis=1)
+    pre[:, 128:3200] = hidden
+    value = jnp.where(mask(0, 128, 3200), hidden * jax.nn.sigmoid(hidden), 0.0).astype(BF16)
+    act[:, 128:3200] = value
+    taps[:, 128:3200] = jnp.dot(w_out[...], value, preferred_element_type=F32)
 
     for t in range(0, PRED_TILES, 2):
         first = (PRED_FIRST + t) * 128
@@ -267,21 +272,12 @@
         send(pred_send.at[device[0]], pred_recv.at[me_m], 2, device)
     pred_recv[me_m] = pred_send[me_m]
 
-    def own_slopes(i, carry):
-        start = pl.multiple_of(384 + i * 256, 128)
-        lanes = pl.ds(start, 256)
-        hidden = pre[:, lanes]
-        gate = jax.nn.sigmoid(hidden)
-        pre[:, lanes] = gate * (1.0 + hidden * (1.0 - gate))
-        row, col = place(0, C, 256)
-        lane = lax.broadcasted_iota(jnp.int32, (C, 256), 1).astype(F32) + start.astype(F32)
-        row = jnp.floor((lane + 0.5) * (1.0 / PITCH))
-        col = lane - PITCH * row
-        own = (row >= HALO) & (row < HALO + ROWS) & (col >= HALO) & (col < HALO + COLS)
-        act_own[:, lanes] = jnp.where(own, act[:, lanes].astype(F32), 0.0).astype(BF16)
-        return carry
-
-    lax.fori_loop(0, 10, own_slopes, 0)
+    hidden = pre[:, 384:2944]
+    gate = jax.nn.sigmoid(hidden)
+    pre[:, 384:2944] = gate * (1.0 + hidden * (1.0 - gate))
+    act_own[:, 384:2944] = jnp.where(
+        mask(1, 384, 2944), act[:, 384:2944].astype(F32), 0.0
+    ).astype(BF16)
     wait_recv(pred_recv.at[pl.ds(0, members - 1)], 2)
 
     coupling = (1.0 - 0.05 / members) / (members - 1)
@@ -301,8 +297,8 @@
                 if 2 * d != members:
                     spread -= jnp.concatenate([term[members - d :], term[: members - d]], axis=0)
             value = slope(own - wanted[None, half * 8 : half * 8 + 8]) - coupling * spread
-            field[:, half * 8 : half * 8 + 8, :] = value
-        grad_send[:, u] = field[...].astype(BF16)
+            grads[:, half * 8 : half * 8 + 8, :] = value
+        grad_send[:, u] = grads[...].astype(BF16)
 
     for dz, h in group_m:
         device = at(dz, h, 0, 0)
@@ -324,33 +320,18 @@
         gc[:, 512:2816], act_own[:, 512:2816], contract_lanes, preferred_element_type=F32
     )
     part_sum[0, 0:PART] = out_part.reshape(PART, 8, C)
-    part_sum[0, PART:] = jnp.zeros((quads * chunk - PART, 8, C), F32)
     for h, da in group_q:
         device = at(0, h, da, 0)
         slot = (device[0] % 2) * lats + device[1]
         send(part_sum.at[0, pl.ds(slot * chunk, chunk)], part_recv.at[0, me_q], 4, device)
 
-    def backward(i, carry):
-        start = pl.multiple_of(384 + i * 256, 128)
-        lanes = pl.ds(start, 256)
-        value = jnp.dot(w_out_t[...], gc[:, lanes], preferred_element_type=F32) * pre[:, lanes]
-        lane = lax.broadcasted_iota(jnp.int32, (C, 256), 1)
-        inside = (lane + start >= low_lane) & (lane + start < high_lane)
-        value = jnp.where(inside, value, 0.0)
-        spread = lane.astype(F32) + start.astype(F32)
-        row = jnp.floor((spread + 0.5) * (1.0 / PITCH))
-        col = spread - PITCH * row
-        own = (row >= HALO) & (row < HALO + ROWS) & (col >= HALO) & (col < HALO + COLS)
-        gh[:, lanes] = jnp.where(own, value, 0.0).astype(BF16)
-        taps[:, lanes] = jnp.dot(w_in_t[...], value.astype(BF16), preferred_element_type=F32)
-        return carry
-
-    lax.fori_loop(0, 10, backward, 0)
+    value = jnp.dot(w_out_t[...], gc[:, 384:2944], preferred_element_type=F32) * pre[:, 384:2944]
+    gh_own[:, 384:2944] = jnp.where(mask(1, 384, 2944), value, 0.0).astype(BF16)
+    gh[:, 384:2944] = jnp.where(mask(0, 384, 2944), value, 0.0).astype(BF16)
     in_part = lax.dot_general(
-        xc[:, 512:2816], gh[:, 512:2816], contract_lanes, preferred_element_type=F32
+        xc[:, 512:2816], gh_own[:, 512:2816], contract_lanes, preferred_element_type=F32
     )
     part_sum[1, 0:PART] = in_part.reshape(PART, 8, C)
-    part_sum[1, PART:] = jnp.zeros((quads * chunk - PART, 8, C), F32)
     for h, da in group_q:
         device = at(0, h, da, 0)
         slot = (device[0] % 2) * lats + device[1]
@@ -358,57 +339,80 @@
     for p in range(2):
         part_recv[p, me_q] = part_sum[p, pl.ds(me_q * chunk, chunk)]
 
+    def total_of(ref, count):
+        total = ref[0]
+        for i in range(1, count):
+            total += ref[i]
+        return total
+
+    def to_lons(p, phase):
+        for d in group_o:
+            send(lon_recv.at[p, me_o], lon_recv.at[p, me_o], phase, at(0, 0, 0, d))
+
+    def to_zs(p, phase):
+        for d in group_z:
+            send(mem_recv.at[p, me_z], mem_recv.at[p, me_z], phase, at(d, 0, 0, 0))
+
+    wait_recv(part_recv.at[0, pl.ds(0, quads - 1)], 4)
+    lon_recv[0, me_o] = total_of(part_recv.at[0], quads)
+    to_lons(0, 6)
+
+    taps[:, 384:2944] = jnp.dot(w_in_t[...], gh[:, 384:2944], preferred_element_type=F32)
     for r in range(ROWS):
         start = PITCH * (r + HALO) + HALO
         total = gp[:, start : start + COLS]
         for k, shift in enumerate(SHIFTS):
             total += taps[k * LEV : (k + 1) * LEV, start - shift : start - shift + COLS]
-        field[:, r, :] = total
-    store = pltpu.make_async_copy(field, field_hbm.at[0], load_sem.at[0])
-    store.start()
-
-    wait_recv(part_recv.at[0, pl.ds(0, quads - 1)], 4)
+        by_row[r] = total
+    for level in range(LEV):
+        field[level] = by_row[:, level, :]
+
     wait_recv(part_recv.at[1, pl.ds(0, quads - 1)], 5)
-    for p in range(2):
-        total = part_recv[p, 0]
-        for q in range(1, quads):
-            total += part_recv[p, q]
-        lon_recv[me_o, pl.ds(p * chunk, chunk)] = total
-    for d in group_o:
-        send(lon_recv.at[me_o], lon_recv.at[me_o], 6, at(0, 0, 0, d))
-    wait_recv(lon_recv.at[pl.ds(0, lons - 1)], 6)
-    total = lon_recv[0]
-    for i in range(1, lons):
-        total += lon_recv[i]
-    mem_recv[me_z] = total
-    for d in group_z:
-        send(mem_recv.at[me_z], mem_recv.at[me_z], 7, at(d, 0, 0, 0))
-    wait_recv(mem_recv.at[pl.ds(0, zs - 1)], 7)
-    total = mem_recv[0]
-    for i in range(1, zs):
-        total += mem_recv[i]
-    all_recv[me_q] = total * (1.0 / math.sqrt(members * lats * lons * ROWS * COLS))
+    mem_recv[1, me_z] = total_of(part_recv.at[1], quads)
+    to_zs(1, 7)
+    wait_recv(lon_recv.at[0, pl.ds(0, lons - 1)], 6)
+    mem_recv[0, me_z] = total_of(lon_recv.at[0], lons)
+    to_zs(0, 8)
+    wait_recv(mem_recv.at[1, pl.ds(0, zs - 1)], 7)
+    lon_recv[1, me_o] = total_of(mem_recv.at[1], zs)
+    to_lons(1, 9)
+    scale = 1.0 / math.sqrt(members * lats * lons * ROWS * COLS)
+    wait_recv(mem_recv.at[0, pl.ds(0, zs - 1)], 8)
+    all_recv[0, me_q] = total_of(mem_recv.at[0], zs) * scale
     for h, da in group_q:
-        send(all_recv.at[me_q], all_recv.at[me_q], 8, at(0, h, da, 0))
-    wait_recv(all_recv.at[pl.ds(0, quads - 1)], 8)
-
-    for t in range(PART):
-        k, half = t // 2, t % 2
-        gout_ref[k, half * 8 : half * 8 + 8, :] = all_recv[t // chunk, t % chunk]
-    for k in range(9):
-        pair = [all_recv[t // chunk, chunk + t % chunk] for t in (2 * k, 2 * k + 1)]
-        gin_ref[k] = jnp.concatenate(pair, axis=0).T
-
-    store.wait()
+        send(all_recv.at[0, me_q], all_recv.at[0, me_q], 10, at(0, h, da, 0))
+    wait_recv(lon_recv.at[1, pl.ds(0, lons - 1)], 9)
+    all_recv[1, me_q] = total_of(lon_recv.at[1], lons) * scale
+    for h, da in group_q:
+        send(all_recv.at[1, me_q], all_recv.at[1, me_q], 11, at(0, h, da, 0))
+
     wait_send(side_recv, 0)
     wait_send(band_recv, 1)
     wait_send(pred_recv.at[pl.ds(0, members - 1)], 2)
     wait_send(grad_recv.at[pl.ds(0, members - 1)], 3)
-    wait_send(part_recv.at[0, pl.ds(0, quads - 1)], 4)
-    wait_send(part_recv.at[1, pl.ds(0, quads - 1)], 5)
-    wait_send(lon_recv.at[pl.ds(0, lons - 1)], 6)
-    wait_send(mem_recv.at[pl.ds(0, zs - 1)], 7)
-    wait_send(all_recv.at[pl.ds(0, quads - 1)], 8)
+    for p in range(2):
+        wait_send(part_recv.at[p, pl.ds(0, quads - 1)], 4 + p)
+        wait_send(lon_recv.at[p, pl.ds(0, lons - 1)], 6 + 3 * p)
+        wait_send(mem_recv.at[p, pl.ds(0, zs - 1)], 8 - p)
+    for p in range(2):
+        wait_recv(all_recv.at[p, pl.ds(0, quads - 1)], 10 + p)
+        for t in range(PART):
+            sums_ref[p, t] = all_recv[p, t // chunk, t % chunk]
+    for p in range(2):
+        wait_send(all_recv.at[p, pl.ds(0, quads - 1)], 10 + p)
+
+
+def write_out(field, sums, field_out, gin_out, gout_out, sem):
+    copies = [
+        pltpu.make_async_copy(src, dst, sem.at[i])
+        for i, (src, dst) in enumerate(
+            ((field, field_out.at[0]), (sums.at[1], gin_out), (sums.at[0], gout_out))
+        )
+    ]
+    for copy in copies:
+        copy.start()
+    for copy in copies:
+        copy.wait()
 
 
 def shards(sizes, inputs, target, conv_in, bias_in, conv_out):
@@ -417,36 +421,28 @@
     share = -(-PRED_TILES // members)
     chunk = -(-PART // quads)
     wide = FLAT + LEAD + 128
-    return pl.pallas_call(
+    anywhere = pl.BlockSpec(memory_space=pl.ANY)
+    near = pl.BlockSpec(memory_space=pltpu.VMEM)
+    field, sums = pl.pallas_call(
         functools.partial(kernel, sizes),
         out_shape=(
-            jax.ShapeDtypeStruct((1, LEV, ROWS, COLS), F32),
-            jax.ShapeDtypeStruct((9, C, LEV), F32),
-            jax.ShapeDtypeStruct((9, LEV, C), F32),
+            pltpu.VMEM((LEV, ROWS, COLS), F32),
+            pltpu.VMEM((2, PART, 8, C), F32),
         ),
-        in_specs=[
-            pl.BlockSpec(memory_space=pl.ANY),
-            pl.BlockSpec(memory_space=pl.ANY),
-            pl.BlockSpec(memory_space=pl.ANY),
-            pl.BlockSpec(memory_space=pltpu.VMEM),
-            pl.BlockSpec(memory_space=pl.ANY),
-        ],
-        out_specs=(
-            pl.BlockSpec(memory_space=pl.ANY),
-            pl.BlockSpec(memory_space=pltpu.VMEM),
-            pl.BlockSpec(memory_space=pltpu.VMEM),
-        ),
+        in_specs=[pl.BlockSpec(memory_space=pltpu.HBM)] * 5,
+        out_specs=(near, near),
         scratch_shapes=[
             pltpu.VMEM((LEV, ROWS, COLS), BF16),
             pltpu.VMEM((LEV, ROWS, COLS), BF16),
-            pltpu.VMEM((9, C, LEV), BF16),
-            pltpu.VMEM((9, LEV, C), BF16),
+            pltpu.VMEM((TAPS, C), BF16),
+            pltpu.VMEM((TAPS, C), BF16),
+            pltpu.VMEM((1, C), F32),
             pltpu.VMEM((2 * LEV, ROWS, COLS), F32),
             pltpu.VMEM((2 * LEV, wide), F32),
             pltpu.VMEM((C, TAPS), BF16),
-            pltpu.VMEM((TAPS, C), BF16),
             pltpu.VMEM((C, TAPS), BF16),
             pltpu.VMEM((C, C), F32),
+            pltpu.VMEM((2, 8, FLAT), F32),
             pltpu.VMEM((2, 2 * LEV, 128), BF16),
             pltpu.VMEM((2, 2 * LEV, 640), BF16),
             pltpu.VMEM((2, 3, 2 * LEV, 128), BF16),
@@ -459,26 +455,53 @@
             pltpu.VMEM((members, share, LEV, 128), BF16),
             pltpu.VMEM((members, share, LEV, 128), BF16),
             pltpu.VMEM((members * share, LEV, 128), F32),
+            pltpu.VMEM((members, LEV, 128), F32),
             pltpu.VMEM((members, share, LEV, 128), BF16),
             pltpu.VMEM((members, share, LEV, 128), BF16),
             pltpu.VMEM((LEV, FLAT), F32),
             pltpu.VMEM((TAPS, FLAT), BF16),
             pltpu.VMEM((C, FLAT), BF16),
-            pltpu.VMEM((LEV, ROWS, COLS), F32),
+            pltpu.VMEM((C, FLAT), BF16),
+            pltpu.VMEM((ROWS, LEV, COLS), F32),
             pltpu.VMEM((2, quads * chunk, 8, C), F32),
             pltpu.VMEM((2, quads, chunk, 8, C), F32),
-            pltpu.VMEM((lons, 2 * chunk, 8, C), F32),
-            pltpu.VMEM((members // 2, 2 * chunk, 8, C), F32),
-            pltpu.VMEM((quads, 2 * chunk, 8, C), F32),
-            pltpu.SemaphoreType.DMA((4,)),
-            pltpu.SemaphoreType.DMA((9,)),
-            pltpu.SemaphoreType.DMA((9,)),
+            pltpu.VMEM((2, lons, chunk, 8, C), F32),
+            pltpu.VMEM((2, members // 2, chunk, 8, C), F32),
+            pltpu.VMEM((2, quads, chunk, 8, C), F32),
+            pltpu.SemaphoreType.DMA((5,)),
+            pltpu.SemaphoreType.DMA((12,)),
+            pltpu.SemaphoreType.DMA((12,)),
         ],
         compiler_params=pltpu.CompilerParams(
-            collective_id=0, has_side_effects=True, vmem_limit_bytes=40 * 1024 * 1024
+            collective_id=0, has_side_effects=True, vmem_limit_bytes=VMEM_LIMIT
         ),
         name="downscaling_step",
-    )(inputs, target, conv_in, bias_in.reshape(1, C), conv_out)
+    )(
+        *(
+            pltpu.with_memory_space_constraint(operand, pltpu.HBM)
+            for operand in (
+                inputs,
+                target,
+                conv_in.transpose(0, 2, 1).reshape(TAPS, C),
+                bias_in.reshape(1, C),
+                conv_out.reshape(TAPS, C),
+            )
+        )
+    )
+    field, gin, gout = pl.pallas_call(
+        write_out,
+        out_shape=(
+            jax.ShapeDtypeStruct((1, LEV, ROWS, COLS), F32),
+            jax.ShapeDtypeStruct((PART, 8, C), F32),
+            jax.ShapeDtypeStruct((PART, 8, C), F32),
+        ),
+        in_specs=[near] * 2,
+        out_specs=(anywhere,) * 3,
+        scratch_shapes=[pltpu.SemaphoreType.DMA((3,))],
+        compiler_params=pltpu.CompilerParams(vmem_limit_bytes=1024 * 1024),
+        name="write_out",
+    )(field, sums)
+    return field, gin.reshape(9, LEV, C).transpose(0, 2, 1), gout.reshape(9, LEV, C)
 
 
 def solution(mesh):

time: 66.7 us -> 54.8 us (0.82)
  Pallas kernels: 62.7 us -> 54 us
  local copies, waits for them, and re-layouts: 3.18 us -> 0 us
    pallas_call x1 -> x2, Pallas kernels: 62.7 us -> 54 us  [the longest x1 53.3 us: shards(): pl.pallas_call(functools.partial(kernel, sizes), out_shape=(pltpu.VMEM((L...]
    unnamed x11 -> x0, local copies, waits for them, and re-layouts: 2.34 us -> none
    pallas_call x1 -> x0, local copies, waits for them, and re-layouts: 0.84 us -> none  [shards(): pl.pallas_call(functools.partial(kernel, sizes), out_shape=(jax.ShapeDtyp...]
where the time goes in v2:
time: 54.8 us; the launch traced here: 54.7 us
  Pallas kernels  54 us (99%)
  between operations  0.64 us (1%)
    pallas_call x1, Pallas kernels, shards(): pl.pallas_call(functools.partial(kernel, sizes), out_shape=(pltpu.VMEM((L...  53.3 us

profile of v2, /device:TPU:1, one launch (start us, length us, event | category | flops | bytes accessed | tf_op | source)
XLA Modules:
  0.0 54.7 jit_solution(13592016252522678072)
XLA Ops:
  0.6 53.3 %downscaling_step.1 = (f32[16,16,128]{2,1,0:T(8,128)S(1)}, f32[2,18,8,128]{3,2,1,0:T(8,128)S(1)}) custom-call(bf16[1,16,16,128]{3,2,1,0:T(8,128)(2,1)} %x_hbm.1, bf16[16,16,128]{2,1,0:T(8,128)(2,1)} %t_hbm.1, bf16[144,128]{1,0:T(8,128)(2,1)} %bitcast.9, f32[1,128]{1,0:T(1,128)} %bitcast.11, bf16[144,128]{1,0:T(8,128)(2,1)} %bitcast.10), custom_call_target="tpu_custom_call" | custom-call | tf_op jit(solution)/shard_map/downscaling_step/pallas_call | solution.py:426
  53.9 0.7 %write_out.1 = (f32[1,16,16,128]{3,2,1,0:T(8,128)}, f32[18,8,128]{2,1,0:T(8,128)}, f32[18,8,128]{2,1,0:T(8,128)}) custom-call(f32[16,16,128]{2,1,0:T(8,128)S(1)} %get-tuple-element.8.field, f32[2,18,8,128]{3,2,1,0:T(8,128)S(1)} %get-tuple-element.9.sums), custom_call_target="tpu_custom_call" | custom-call | tf_op jit(solution)/shard_map/write_out/pallas_call | solution.py:491

commit v3 on v2

--- a/solution.py
+++ b/solution.py
@@ -81,6 +81,7 @@
     load_sem,
     send_sem,
     recv_sem,
+    met_sem,
 ):
     members, lats, lons = sizes
     zs = members // 2
@@ -123,12 +124,19 @@
     group_z = [d for d in ring_order(zs) if d]
 
     barrier = pltpu.get_barrier_semaphore()
-    greet = [at(dz, h, 0, 0) for dz, h in group_m]
-    greet += [at(0, 0, 0, d) for d in group_o]
-    greet += [at(0, h, da, 0) for h, da in group_q]
-    greet += [at(0, 0, da, do) for da, do in halo]
-    for device in greet:
+    near = [at(0, 0, da, do) for da, do in halo] + [at(1, 0, 0, 0), at(zs - 1, 0, 0, 0), at(0, 1, 0, 0)]
+    for device in near:
         pl.semaphore_signal(barrier, inc=1, device_id=device, device_id_type=MESH)
+
+    steps = [at(1, 0, 0, 0), at(zs - 1, 0, 0, 0), at(0, 1, 0, 0)]
+    steps += [at(0, 0, da, do) for da, do in halo if da == 0 or do == 0]
+
+    def tell(wave):
+        for device in steps:
+            pl.semaphore_signal(met_sem.at[wave], inc=1, device_id=device, device_id_type=MESH)
+
+    def hear(wave):
+        pl.semaphore_wait(met_sem.at[wave], len(steps))
 
     loads[0].wait()
     loads[1].wait()
@@ -156,7 +164,7 @@
     band_send[0] = xf[:, LEAD + 17 * 128 : LEAD + 22 * 128].astype(BF16)
     band_send[1] = xf[:, LEAD + 4 * 128 : LEAD + 9 * 128].astype(BF16)
 
-    pl.semaphore_wait(barrier, len(greet))
+    pl.semaphore_wait(barrier, len(near))
 
     def send(src, dst, phase, device):
         copy = pltpu.make_async_remote_copy(
@@ -195,11 +203,15 @@
     send(band_send.at[0], band_recv.at[0], 1, at(0, 0, 1, 0))
     send(band_send.at[1], band_recv.at[1], 1, at(0, 0, -1, 0))
 
+    tell(0)
+
     for load in loads[2:]:
         load.wait()
     w_in[...] = w_in_t[...].astype(F32).T.astype(BF16)
     w_out_t[...] = w_out[...].astype(F32).T.astype(BF16)
     bias[...] = jnp.broadcast_to(bias16[...], (C, C)).T
+    hear(0)
+    tell(1)
     taps[:, 0:128] = jnp.zeros((TAPS, 128), F32)
     taps[:, FLAT - 128 : FLAT] = jnp.zeros((TAPS, 128), F32)
     xf[:, 0:LEAD] = jnp.zeros((2 * LEV, LEAD), F32)
@@ -220,6 +232,8 @@
         (row >= HALO) & (row < HALO + ROWS) & (col >= HALO) & (col < HALO + COLS), 1.0, 0.0
     )
 
+    hear(1)
+    tell(2)
     wait_recv(side_recv, 0)
     wait_recv(band_recv, 1)
 
@@ -246,6 +260,9 @@
         if PRED_FIRST <= t < PRED_FIRST + PRED_TILES:
             target_tiles[t - PRED_FIRST] = tile[LEV:]
 
+    hear(2)
+    tell(3)
+
     for k, shift in enumerate(SHIFTS):
         xc[k * LEV : (k + 1) * LEV, 128:3200] = xf[0:LEV, LEAD + 128 + shift : LEAD + 3200 + shift].astype(BF16)
 
@@ -267,6 +284,7 @@
         for u in (t, t + 1):
             pred_send[u % members, u // members] = total[:, (u - t) * 128 : (u - t + 1) * 128].astype(BF16)
 
+    hear(3)
     for dz, h in group_m:
         device = at(dz, h, 0, 0)
         send(pred_send.at[device[0]], pred_recv.at[me_m], 2, device)
@@ -471,6 +489,7 @@
             pltpu.SemaphoreType.DMA((5,)),
             pltpu.SemaphoreType.DMA((12,)),
             pltpu.SemaphoreType.DMA((12,)),
+            pltpu.SemaphoreType.REGULAR((4,)),
         ],
         compiler_params=pltpu.CompilerParams(
             collective_id=0, has_side_effects=True, vmem_limit_bytes=VMEM_LIMIT

time: 54.8 us -> 54.4 us (level)
  no operation moved by 1% of the time
where the time goes in v3:
time: 54.4 us; the launch traced here: 54.3 us
  Pallas kernels  53.6 us (99%)
  between operations  0.64 us (1%)
    pallas_call x1, Pallas kernels, shards(): pl.pallas_call(functools.partial(kernel, sizes), out_shape=(pltpu.VMEM((L...  52.9 us

profile of v3, /device:TPU:1, one launch (start us, length us, event | category | flops | bytes accessed | tf_op | source)
XLA Modules:
  0.0 54.3 jit_solution(9522988512082101689)
XLA Ops:
  0.6 52.9 %downscaling_step.1 = (f32[16,16,128]{2,1,0:T(8,128)S(1)}, f32[2,18,8,128]{3,2,1,0:T(8,128)S(1)}) custom-call(bf16[1,16,16,128]{3,2,1,0:T(8,128)(2,1)} %x_hbm.1, bf16[16,16,128]{2,1,0:T(8,128)(2,1)} %t_hbm.1, bf16[144,128]{1,0:T(8,128)(2,1)} %bitcast.9, f32[1,128]{1,0:T(1,128)} %bitcast.11, bf16[144,128]{1,0:T(8,128)(2,1)} %bitcast.10), custom_call_target="tpu_custom_call" | custom-call | tf_op jit(solution)/shard_map/downscaling_step/pallas_call | solution.py:444
  53.6 0.7 %write_out.1 = (f32[1,16,16,128]{3,2,1,0:T(8,128)}, f32[18,8,128]{2,1,0:T(8,128)}, f32[18,8,128]{2,1,0:T(8,128)}) custom-call(f32[16,16,128]{2,1,0:T(8,128)S(1)} %get-tuple-element.8.field, f32[2,18,8,128]{3,2,1,0:T(8,128)S(1)} %get-tuple-element.9.sums), custom_call_target="tpu_custom_call" | custom-call | tf_op jit(solution)/shard_map/write_out/pallas_call | solution.py:510

commit v4 on v3

v4 whole, which is shorter than its diff:
```python
import functools
import math

import jax
import jax.numpy as jnp
from jax import lax
from jax.experimental import pallas as pl
from jax.experimental.pallas import tpu as pltpu
from jax.sharding import PartitionSpec as P

MESH = pl.DeviceIdType.MESH
F32 = jnp.float32
BF16 = jnp.bfloat16
SUM = jnp.bfloat16

LEV = 16
C = 128
ROWS = 16
COLS = 128
HALO = 4
PITCH = COLS + 2 * HALO
FLAT = 26 * 128
LEAD = 128
OFFSETS = [(di, dj) for di in (-1, 0, 1) for dj in (-1, 0, 1)]
SHIFTS = [di * PITCH + dj for di, dj in OFFSETS]
PRED_FIRST = 2
PRED_TILES = 22
TAPS = 9 * LEV
VMEM_LIMIT = 40 * 1024 * 1024


def ring_order(count):
    return sorted(range(count), key=lambda d: (-min(d, count - d), d))


def shares(members):
    share = max(2, -(-PRED_TILES // members))
    return share, -(-PRED_TILES // share)


def kernel(
    sizes,
    x_hbm,
    t_hbm,
    w_in_hbm,
    bias_ref,
    w_out_hbm,
    field,
    sums_ref,
    x16,
    t16,
    w_in_t,
    w_out,
    bias16,
    rows32,
    xf,
    w_in,
    w_out_t,
    bias,
    masks,
    side_send,
    band_send,
    side_recv,
    band_recv,
    xc,
    pre,
    act,
    act_own,
    taps,
    pred_send,
    pred_recv,
    target_tiles,
    grads,
    grad_send,
    grad_recv,
    gp,
    gc,
    gh,
    gh_own,
    by_row,
    part_sum,
    part_recv,
    spare_recv,
    lon_recv,
    mem_recv,
    all_recv,
    load_sem,
    send_sem,
    recv_sem,
    met_sem,
):
    members, lats, lons = sizes
    zs = members // 2
    quads = 2 * lats
    share, owners = shares(members)
    me_m = lax.axis_index("member")
    me_a = lax.axis_index("lat")
    me_o = lax.axis_index("lon")
    me_z = me_m // 2
    me_h = me_m % 2
    me_q = me_h * lats + me_a

    loads = [
        pltpu.make_async_copy(src, dst, load_sem.at[i])
        for i, (src, dst) in enumerate(
            (
                (x_hbm.at[0], x16),
                (t_hbm, t16),
                (w_in_hbm, w_in_t),
                (w_out_hbm, w_out),
                (bias_ref, bias16),
            )
        )
    ]
    for load in loads:
        load.start()

    def at(dm_z, dm_h, da, do):
        return (
            ((me_z + dm_z) % zs) * 2 + (me_h + dm_h) % 2,
            (me_a + da + lats) % lats,
            (me_o + do + lons) % lons,
        )

    halo = [(da, do) for da, do in ((-1, -1), (-1, 1), (1, -1), (1, 1), (0, -1), (0, 1), (-1, 0), (1, 0))]
    group_m = [(dz, h) for dz in ring_order(zs) for h in (1, 0) if dz or h]
    group_q = [(1, 0), (1, 1), (1, 3), (1, 2), (0, 2), (0, 1), (0, 3)]
    group_o = [d for d in ring_order(lons) if d]
    group_z = [d for d in ring_order(zs) if d]

    barrier = pltpu.get_barrier_semaphore()
    near = [at(0, 0, da, do) for da, do in halo] + [at(0, 1, 0, 0)]
    near += [at(dz, 0, 0, 0) for dz in (1, zs - 1, 2, zs - 2)] + [at(0, 0, 0, do) for do in (2, -2)]
    for device in near:
        pl.semaphore_signal(barrier, inc=1, device_id=device, device_id_type=MESH)

    steps = [at(dz, 0, 0, 0) for dz in (2, zs - 2, 1, zs - 1)] + [at(0, 0, 0, do) for do in (2, -2)]
    steps += [at(0, 0, da, 0) for da in (1, -1)]

    def tell(wave):
        for device in steps:
            pl.semaphore_signal(met_sem.at[wave], inc=1, device_id=device, device_id_type=MESH)

    def hear(wave):
        pl.semaphore_wait(met_sem.at[wave], len(steps))

    loads[0].wait()
    loads[1].wait()
    rows32[0:LEV] = x16[...].astype(F32)
    rows32[LEV:] = t16[...].astype(F32)
    for r in range(ROWS):
        start = LEAD + PITCH * (r + HALO) + HALO
        xf[:, start : start + COLS] = rows32[:, r, :]

    def place(first, height, width):
        lane = lax.broadcasted_iota(jnp.int32, (height, width), 1).astype(F32) + float(first)
        row = jnp.floor((lane + 0.5) * (1.0 / PITCH))
        return row, lane - PITCH * row

    for part in range(2):
        chans = slice(part * LEV, (part + 1) * LEV)
        left_edge = jnp.zeros((LEV, 128), F32)
        right_edge = jnp.zeros((LEV, 128), F32)
        for t in range(4, 22):
            row, col = place(t * 128, LEV, 128)
            here = (row >= HALO) & (row < HALO + ROWS)
            tile = xf[chans, LEAD + t * 128 : LEAD + t * 128 + 128]
            left_edge += jnp.where(here & (col >= HALO) & (col < 2 * HALO), tile, 0.0)
            right_edge += jnp.where(here & (col >= COLS) & (col < COLS + HALO), tile, 0.0)
        side_send[part, 0] = right_edge.astype(BF16)
        side_send[part, 1] = left_edge.astype(BF16)
        band_send[part, 0] = xf[chans, LEAD + 17 * 128 : LEAD + 22 * 128].astype(BF16)
        band_send[part, 1] = xf[chans, LEAD + 4 * 128 : LEAD + 9 * 128].astype(BF16)

    pl.semaphore_wait(barrier, len(near))

    def send(src, dst, phase, device):
        copy = pltpu.make_async_remote_copy(
            src_ref=src,
            dst_ref=dst,
            send_sem=send_sem.at[phase],
            recv_sem=recv_sem.at[phase],
            device_id=device,
            device_id_type=MESH,
        )
        copy.start()

    def wait_recv(ref, phase):
        pltpu.make_async_remote_copy(
            src_ref=ref,
            dst_ref=ref,
            send_sem=send_sem.at[phase],
            recv_sem=recv_sem.at[phase],
            device_id=(me_m, me_a, (me_o + 1) % lons),
            device_id_type=MESH,
        ).wait_recv()

    def wait_send(ref, phase):
        pltpu.make_async_remote_copy(
            src_ref=ref,
            dst_ref=ref,
            send_sem=send_sem.at[phase],
            recv_sem=recv_sem.at[phase],
            device_id=(me_m, me_a, (me_o + 1) % lons),
            device_id_type=MESH,
        ).wait_send()

    for part in range(2):
        for da in (-1, 1, 0):
            send(side_send.at[part, 0], side_recv.at[part, 0, 1 - da], 2 * part, at(0, 0, da, 1))
            send(side_send.at[part, 1], side_recv.at[part, 1, 1 - da], 2 * part, at(0, 0, da, -1))
        send(band_send.at[part, 0], band_recv.at[part, 0], 2 * part + 1, at(0, 0, 1, 0))
        send(band_send.at[part, 1], band_recv.at[part, 1], 2 * part + 1, at(0, 0, -1, 0))
    tell(0)

    for load in loads[2:]:
        load.wait()
    w_in[...] = w_in_t[...].astype(F32).T.astype(BF16)
    w_out_t[...] = w_out[...].astype(F32).T.astype(BF16)
    bias[...] = jnp.broadcast_to(bias16[...], (C, C)).T
    taps[:, 0:128] = jnp.zeros((TAPS, 128), F32)
    taps[:, FLAT - 128 : FLAT] = jnp.zeros((TAPS, 128), F32)
    xf[:, 0:LEAD] = jnp.zeros((2 * LEV, LEAD), F32)
    xf[:, LEAD + FLAT :] = jnp.zeros((2 * LEV, 128), F32)
    gp[:, 0 : PRED_FIRST * 128] = jnp.zeros((LEV, PRED_FIRST * 128), F32)
    gp[:, (PRED_FIRST + PRED_TILES) * 128 :] = jnp.zeros((LEV, PRED_FIRST * 128), F32)
    for u in range(PRED_TILES, owners * share):
        target_tiles[u] = jnp.zeros((LEV, 128), F32)
        pred_send[u % owners, u // owners] = jnp.zeros((LEV, 128), BF16)
    lon_recv[me_o, 2] = jnp.zeros((LEV, C), SUM)
    row_low = jnp.where(me_a == 0, HALO, 0).astype(F32)
    row_high = jnp.where(me_a == lats - 1, HALO + ROWS, ROWS + 2 * HALO).astype(F32)
    row, col = place(0, 8, FLAT)
    masks[0] = jnp.where((row >= row_low) & (row < row_high), 1.0, 0.0)
    masks[1] = jnp.where(
        (row >= HALO) & (row < HALO + ROWS) & (col >= HALO) & (col < HALO + COLS), 1.0, 0.0
    )

    hear(0)
    tell(1)
    wait_recv(side_recv.at[0], 0)
    wait_recv(band_recv.at[0], 1)

    def unpack(part):
        chans = slice(part * LEV, (part + 1) * LEV)
        sides = [[side_recv[part, i, j].astype(F32) for j in range(3)] for i in range(2)]
        for t in range(26):
            row, col = place(t * 128, LEV, 128)
            lanes = slice(LEAD + t * 128, LEAD + t * 128 + 128)
            tile = xf[chans, lanes]
            left, right = sides[0][1], sides[1][1]
            if t < 5:
                above = row < HALO
                band = band_recv[part, 0, :, t * 128 : t * 128 + 128].astype(F32)
                tile = jnp.where(above, band, tile)
                left = jnp.where(above, sides[0][0], left)
                right = jnp.where(above, sides[1][0], right)
            if t >= 21:
                below = row >= HALO + ROWS
                band = band_recv[part, 1, :, (t - 21) * 128 : (t - 20) * 128].astype(F32)
                tile = jnp.where(below, band, tile)
                left = jnp.where(below, sides[0][2], left)
                right = jnp.where(below, sides[1][2], right)
            tile = jnp.where(col < HALO, left, tile)
            tile = jnp.where(col >= HALO + COLS, right, tile)
            if t < 5 or t >= 21:
                tile = jnp.where((row >= row_low) & (row < row_high), tile, 0.0)
            if part == 0:
                xf[chans, lanes] = tile
            elif PRED_FIRST <= t < PRED_FIRST + PRED_TILES:
                target_tiles[t - PRED_FIRST] = tile

    unpack(0)
    for k, shift in enumerate(SHIFTS):
        xc[k * LEV : (k + 1) * LEV, 128:3200] = xf[0:LEV, LEAD + 128 + shift : LEAD + 3200 + shift].astype(BF16)

    def mask(which, first, last):
        return masks[which, 0:1, first:last] > 0.5

    hidden = jnp.dot(w_in[...], xc[:, 128:3200], preferred_element_type=F32)
    hidden += jnp.concatenate([bias[...]] * 24, axis=1)
    pre[:, 128:3200] = hidden
    value = jnp.where(mask(0, 128, 3200), hidden * jax.nn.sigmoid(hidden), 0.0).astype(BF16)
    act[:, 128:3200] = value
    taps[:, 128:3200] = jnp.dot(w_out[...], value, preferred_element_type=F32)

    for t in range(0, PRED_TILES, 11):
        first, width = (PRED_FIRST + t) * 128, 11 * 128
        total = xf[0:LEV, LEAD + first : LEAD + first + width]
        for k, shift in enumerate(SHIFTS):
            total += taps[k * LEV : (k + 1) * LEV, first + shift : first + shift + width]
        for u in range(11):
            pred_send[(t + u) % owners, (t + u) // owners] = total[:, u * 128 : (u + 1) * 128].astype(BF16)

    hear(1)
    def rank(z, h):
        return ((z - zs + 3 + zs) % zs) * 2 + h

    me_r = rank(me_z, me_h)
    for dz, h in group_m:
        device = at(dz, h, 0, 0)
        slot = rank(device[0] // 2, device[0] % 2)

        @pl.when(slot < owners)
        def _(device=device, slot=slot):
            send(pred_send.at[slot], pred_recv.at[me_m], 4, device)

    hidden = pre[:, 384:2944]
    gate = jax.nn.sigmoid(hidden)
    pre[:, 384:2944] = gate * (1.0 + hidden * (1.0 - gate))
    act_own[:, 384:2944] = jnp.where(
        mask(1, 384, 2944), act[:, 384:2944].astype(F32), 0.0
    ).astype(BF16)
    wait_recv(side_recv.at[1], 2)
    wait_recv(band_recv.at[1], 3)
    unpack(1)

    coupling = (1.0 - 0.05 / members) / (members - 1)

    def slope(d):
        return d * lax.rsqrt(d * d + 0.25)

    @pl.when(me_r < owners)
    def _():
        pred_recv[me_m] = pred_send[me_r]
        wait_recv(pred_recv.at[pl.ds(0, members - 1)], 4)
        for u in range(share):
            everyone = pred_recv[:, u].astype(F32)
            wanted = target_tiles[me_r + u * owners]
            for half in range(2):
                own = everyone[:, half * 8 : half * 8 + 8]
                spread = jnp.zeros_like(own)
                for d in range(1, members // 2 + 1):
                    term = slope(own - jnp.concatenate([own[d:], own[:d]], axis=0))
                    spread += term
                    if 2 * d != members:
                        spread -= jnp.concatenate([term[members - d :], term[: members - d]], axis=0)
                value = slope(own - wanted[None, half * 8 : half * 8 + 8]) - coupling * spread
                grads[:, half * 8 : half * 8 + 8, :] = value
            grad_send[:, u] = grads[...].astype(BF16)
        for dz, h in group_m:
            device = at(dz, h, 0, 0)
            send(grad_send.at[device[0]], grad_recv.at[me_r], 5, device)
        grad_recv[me_r] = grad_send[me_m]
        wait_recv(grad_recv.at[pl.ds(0, owners - 1)], 5)

    @pl.when(me_r >= owners)
    def _():
        wait_recv(grad_recv, 5)

    for u in range(PRED_TILES):
        t = PRED_FIRST + u
        row, col = place(t * 128, LEV, 128)
        inside = (row >= row_low) & (row < row_high) & (col >= HALO - 2) & (col < HALO + COLS + 2)
        tile = grad_recv[u % owners, u // owners].astype(F32)
        gp[:, t * 128 : t * 128 + 128] = jnp.where(inside, tile, 0.0)
    for k, shift in enumerate(SHIFTS):
        gc[k * LEV : (k + 1) * LEV, 384:2944] = gp[:, 384 - shift : 2944 - shift].astype(BF16)

    spare_owner = (0, quads - 1)

    def in_group(q):
        return (me_z * 2 + q // lats, q % lats, me_o)

    def spread_part(p, value):
        part_sum[p] = value.reshape(9, LEV, C).astype(SUM)
        for h, da in group_q:
            device = at(0, h, da, 0)
            slot = (device[0] % 2) * lats + device[1]
            send(part_sum.at[p, slot], part_recv.at[p, me_q], 6 + p, device)

        @pl.when(me_q != spare_owner[p])
        def _():
            send(part_sum.at[p, 8], spare_recv.at[me_q], 8 + p, in_group(spare_owner[p]))

        part_recv[p, me_q] = part_sum[p, me_q]

    def total_of(ref, count):
        total = ref[0].astype(F32)
        for i in range(1, count):
            total += ref[i].astype(F32)
        return total

    contract_lanes = (((1,), (1,)), ((), ()))
    out_part = lax.dot_general(
        gc[:, 512:2816], act_own[:, 512:2816], contract_lanes, preferred_element_type=F32
    )
    spread_part(0, out_part)

    value = jnp.dot(w_out_t[...], gc[:, 384:2944], preferred_element_type=F32) * pre[:, 384:2944]
    gh_own[:, 384:2944] = jnp.where(mask(1, 384, 2944), value, 0.0).astype(BF16)
    gh[:, 384:2944] = jnp.where(mask(0, 384, 2944), value, 0.0).astype(BF16)
    in_part = lax.dot_general(
        xc[:, 512:2816], gh_own[:, 512:2816], contract_lanes, preferred_element_type=F32
    )
    spread_part(1, in_part)

    taps[:, 384:2944] = jnp.dot(w_in_t[...], gh[:, 384:2944], preferred_element_type=F32)
    for r in range(ROWS):
        start = PITCH * (r + HALO) + HALO
        total = gp[:, start : start + COLS]
        for k, shift in enumerate(SHIFTS):
            total += taps[k * LEV : (k + 1) * LEV, start - shift : start - shift + COLS]
        by_row[r] = total

    for p in range(2):
        wait_recv(part_recv.at[p, pl.ds(0, quads - 1)], 6 + p)
        lon_recv[me_o, p] = total_of(part_recv.at[p], quads).astype(SUM)
        others = spare_recv.at[pl.ds(0, quads - 1)]

        @pl.when(me_q == spare_owner[p])
        def _():
            spare_recv[me_q] = part_sum[p, 8]
            wait_recv(others, 8 + p)
            lon_recv[me_o, 2] = total_of(spare_recv, quads).astype(SUM)

    for d in group_o:
        send(lon_recv.at[me_o], lon_recv.at[me_o], 10, at(0, 0, 0, d))
    for level in range(LEV):
        field[level] = by_row[:, level, :]
    wait_recv(lon_recv.at[pl.ds(0, lons - 1)], 10)
    mem_recv[me_z] = total_of(lon_recv, lons).astype(SUM)
    for d in group_z:
        send(mem_recv.at[me_z], mem_recv.at[me_z], 11, at(d, 0, 0, 0))
    scale = 1.0 / math.sqrt(members * lats * lons * ROWS * COLS)
    wait_recv(mem_recv.at[pl.ds(0, zs - 1)], 11)
    all_recv[me_q] = (total_of(mem_recv, zs) * scale).astype(SUM)
    for h, da in group_q:
        send(all_recv.at[me_q], all_recv.at[me_q], 12, at(0, h, da, 0))

    for part in range(2):
        wait_send(side_recv.at[part], 2 * part)
        wait_send(band_recv.at[part], 2 * part + 1)
    @pl.when(me_r < owners)
    def _():
        wait_send(pred_send.at[pl.ds(0, owners - 1)], 4)
        wait_send(grad_send.at[pl.ds(0, members - 1)], 5)

    @pl.when(me_r >= owners)
    def _():
        wait_send(pred_send, 4)

    for p in range(2):
        wait_send(part_recv.at[p, pl.ds(0, quads - 1)], 6 + p)

        @pl.when(me_q != spare_owner[p])
        def _():
            wait_send(spare_recv.at[0], 8 + p)

    wait_send(lon_recv.at[pl.ds(0, lons - 1)], 10)
    wait_send(mem_recv.at[pl.ds(0, zs - 1)], 11)
    wait_recv(all_recv.at[pl.ds(0, quads - 1)], 12)
    for p in range(2):
        for t in range(9):
            value = all_recv[t, p] if t < 8 else all_recv[spare_owner[p], 2]
            sums_ref[p, t] = value.astype(F32)
    wait_send(all_recv.at[pl.ds(0, quads - 1)], 12)


def write_out(field, sums, field_out, gin_out, gout_out, sem):
    copies = [
        pltpu.make_async_copy(src, dst, sem.at[i])
        for i, (src, dst) in enumerate(
            ((field, field_out.at[0]), (sums.at[1], gin_out), (sums.at[0], gout_out))
        )
    ]
    for copy in copies:
        copy.start()
    for copy in copies:
        copy.wait()


def shards(sizes, inputs, target, conv_in, bias_in, conv_out):
    members, lats, lons = sizes
    quads = 2 * lats
    share, owners = shares(members)
    wide = FLAT + LEAD + 128
    anywhere = pl.BlockSpec(memory_space=pl.ANY)
    near = pl.BlockSpec(memory_space=pltpu.VMEM)
    field, sums = pl.pallas_call(
        functools.partial(kernel, sizes),
        out_shape=(
            pltpu.VMEM((LEV, ROWS, COLS), F32),
            pltpu.VMEM((2, 9, LEV, C), F32),
        ),
        in_specs=[pl.BlockSpec(memory_space=pltpu.HBM)] * 5,
        out_specs=(near, near),
        scratch_shapes=[
            pltpu.VMEM((LEV, ROWS, COLS), BF16),
            pltpu.VMEM((LEV, ROWS, COLS), BF16),
            pltpu.VMEM((TAPS, C), BF16),
            pltpu.VMEM((TAPS, C), BF16),
            pltpu.VMEM((1, C), F32),
            pltpu.VMEM((2 * LEV, ROWS, COLS), F32),
            pltpu.VMEM((2 * LEV, wide), F32),
            pltpu.VMEM((C, TAPS), BF16),
            pltpu.VMEM((C, TAPS), BF16),
            pltpu.VMEM((C, C), F32),
            pltpu.VMEM((2, 8, FLAT), F32),
            pltpu.VMEM((2, 2, LEV, 128), BF16),
            pltpu.VMEM((2, 2, LEV, 640), BF16),
            pltpu.VMEM((2, 2, 3, LEV, 128), BF16),
            pltpu.VMEM((2, 2, LEV, 640), BF16),
            pltpu.VMEM((TAPS, FLAT), BF16),
            pltpu.VMEM((C, FLAT), F32),
            pltpu.VMEM((C, FLAT), BF16),
            pltpu.VMEM((C, FLAT), BF16),
            pltpu.VMEM((TAPS, FLAT), F32),
            pltpu.VMEM((owners, share, LEV, 128), BF16),
            pltpu.VMEM((members, share, LEV, 128), BF16),
            pltpu.VMEM((owners * share, LEV, 128), F32),
            pltpu.VMEM((members, LEV, 128), F32),
            pltpu.VMEM((members, share, LEV, 128), BF16),
            pltpu.VMEM((owners, share, LEV, 128), BF16),
            pltpu.VMEM((LEV, FLAT), F32),
            pltpu.VMEM((TAPS, FLAT), BF16),
            pltpu.VMEM((C, FLAT), BF16),
            pltpu.VMEM((C, FLAT), BF16),
            pltpu.VMEM((ROWS, LEV, COLS), F32),
            pltpu.VMEM((2, 9, LEV, C), SUM),
            pltpu.VMEM((2, quads, LEV, C), SUM),
            pltpu.VMEM((quads, LEV, C), SUM),
            pltpu.VMEM((lons, 3, LEV, C), SUM),
            pltpu.VMEM((members // 2, 3, LEV, C), SUM),
            pltpu.VMEM((quads, 3, LEV, C), SUM),
            pltpu.SemaphoreType.DMA((5,)),
            pltpu.SemaphoreType.DMA((13,)),
            pltpu.SemaphoreType.DMA((13,)),
            pltpu.SemaphoreType.REGULAR((2,)),
        ],
        compiler_params=pltpu.CompilerParams(
            collective_id=0, has_side_effects=True, vmem_limit_bytes=VMEM_LIMIT
        ),
        name="downscaling_step",
    )(
        *(
            pltpu.with_memory_space_constraint(operand, pltpu.HBM)
            for operand in (
                inputs,
                target,
                conv_in.transpose(0, 2, 1).reshape(TAPS, C),
                bias_in.reshape(1, C),
                conv_out.reshape(TAPS, C),
            )
        )
    )
    field, gin, gout = pl.pallas_call(
        write_out,
        out_shape=(
            jax.ShapeDtypeStruct((1, LEV, ROWS, COLS), F32),
            jax.ShapeDtypeStruct((9, LEV, C), F32),
            jax.ShapeDtypeStruct((9, LEV, C), F32),
        ),
        in_specs=[near] * 2,
        out_specs=(anywhere,) * 3,
        scratch_shapes=[pltpu.SemaphoreType.DMA((3,))],
        compiler_params=pltpu.CompilerParams(vmem_limit_bytes=1024 * 1024),
        name="write_out",
    )(field, sums)
    return field, gin.transpose(0, 2, 1), gout


def solution(mesh):
    sizes = tuple(mesh.shape[axis] for axis in ("member", "lat", "lon"))
    in_specs = (P("member", None, "lat", "lon"), P(None, "lat", "lon"), P(), P(), P())
    out_specs = (P("member", None, "lat", "lon"), P(), P())
    return jax.shard_map(
        functools.partial(shards, sizes),
        mesh=mesh,
        in_specs=in_specs,
        out_specs=out_specs,
        check_vma=False,
    )
```

time: 54.4 us -> 51.5 us (0.947)
  Pallas kernels: 53.6 us -> 50.7 us
    pallas_call x1, Pallas kernels: 52.9 us -> 50 us  [shards(): pl.pallas_call(functools.partial(kernel, sizes), out_shape=(pltpu.VMEM((L...]
where the time goes in v4:
time: 51.5 us; the launch traced here: 51.4 us
  Pallas kernels  50.7 us (98%)
  between operations  0.64 us (1%)
    pallas_call x1, Pallas kernels, shards(): pl.pallas_call(functools.partial(kernel, sizes), out_shape=(pltpu.VMEM((L...  50 us

profile of v4, /device:TPU:1, one launch (start us, length us, event | category | flops | bytes accessed | tf_op | source)
XLA Modules:
  0.0 51.4 jit_solution(5765135970329280277)
XLA Ops:
  0.6 50.0 %downscaling_step.1 = (f32[16,16,128]{2,1,0:T(8,128)S(1)}, f32[2,9,16,128]{3,2,1,0:T(8,128)S(1)}) custom-call(bf16[1,16,16,128]{3,2,1,0:T(8,128)(2,1)} %x_hbm.1, bf16[16,16,128]{2,1,0:T(8,128)(2,1)} %t_hbm.1, bf16[144,128]{1,0:T(8,128)(2,1)} %bitcast.6, f32[1,128]{1,0:T(1,128)} %bitcast.8, bf16[144,128]{1,0:T(8,128)(2,1)} %bitcast.7), custom_call_target="tpu_custom_call" | custom-call | tf_op jit(solution)/shard_map/downscaling_step/pallas_call | solution.py:480
  50.6 0.7 %write_out.1 = (f32[1,16,16,128]{3,2,1,0:T(8,128)}, f32[9,16,128]{2,1,0:T(8,128)}, f32[9,16,128]{2,1,0:T(8,128)}) custom-call(f32[16,16,128]{2,1,0:T(8,128)S(1)} %get-tuple-element.8.field, f32[2,9,16,128]{3,2,1,0:T(8,128)S(1)} %get-tuple-element.9.sums), custom_call_target="tpu_custom_call" | custom-call | tf_op jit(solution)/shard_map/write_out/pallas_call | solution.py:547

commit v5 on v4

--- a/solution.py
+++ b/solution.py
@@ -34,8 +34,8 @@
 
 
 def shares(members):
-    share = max(2, -(-PRED_TILES // members))
-    return share, -(-PRED_TILES // share)
+    low, extra = divmod(PRED_TILES, members)
+    return low, extra
 
 
 def kernel(
@@ -65,7 +65,8 @@
     xc,
     pre,
     act,
-    act_own,
+    act_t,
+    xc_t,
     taps,
     pred_send,
     pred_recv,
@@ -81,8 +82,11 @@
     part_sum,
     part_recv,
     spare_recv,
-    lon_recv,
-    mem_recv,
+    first,
+    second,
+    spare_first,
+    spare_second,
+    spare_all,
     all_recv,
     load_sem,
     send_sem,
@@ -92,7 +96,8 @@
     members, lats, lons = sizes
     zs = members // 2
     quads = 2 * lats
-    share, owners = shares(members)
+    low, extra = shares(members)
+    share = low + 1
     me_m = lax.axis_index("member")
     me_a = lax.axis_index("lat")
     me_o = lax.axis_index("lon")
@@ -224,10 +229,6 @@
     xf[:, LEAD + FLAT :] = jnp.zeros((2 * LEV, 128), F32)
     gp[:, 0 : PRED_FIRST * 128] = jnp.zeros((LEV, PRED_FIRST * 128), F32)
     gp[:, (PRED_FIRST + PRED_TILES) * 128 :] = jnp.zeros((LEV, PRED_FIRST * 128), F32)
-    for u in range(PRED_TILES, owners * share):
-        target_tiles[u] = jnp.zeros((LEV, 128), F32)
-        pred_send[u % owners, u // owners] = jnp.zeros((LEV, 128), BF16)
-    lon_recv[me_o, 2] = jnp.zeros((LEV, C), SUM)
     row_low = jnp.where(me_a == 0, HALO, 0).astype(F32)
     row_high = jnp.where(me_a == lats - 1, HALO + ROWS, ROWS + 2 * HALO).astype(F32)
     row, col = place(0, 8, FLAT)
@@ -285,32 +286,46 @@
     taps[:, 128:3200] = jnp.dot(w_out[...], value, preferred_element_type=F32)
 
     for t in range(0, PRED_TILES, 11):
-        first, width = (PRED_FIRST + t) * 128, 11 * 128
-        total = xf[0:LEV, LEAD + first : LEAD + first + width]
+        begin, width = (PRED_FIRST + t) * 128, 11 * 128
+        total = xf[0:LEV, LEAD + begin : LEAD + begin + width]
         for k, shift in enumerate(SHIFTS):
-            total += taps[k * LEV : (k + 1) * LEV, first + shift : first + shift + width]
+            total += taps[k * LEV : (k + 1) * LEV, begin + shift : begin + shift + width]
         for u in range(11):
-            pred_send[(t + u) % owners, (t + u) // owners] = total[:, u * 128 : (u + 1) * 128].astype(BF16)
+            pred_send[t + u] = total[:, u * 128 : (u + 1) * 128].astype(BF16)
 
     hear(1)
     def rank(z, h):
-        return ((z - zs + 3 + zs) % zs) * 2 + h
+        return ((z + 3) % zs) * 2 + h
+
+    def tiles_of(ref, slot, more):
+        start = slot * share if more else extra + slot * low
+        return ref.at[pl.ds(start, share if more else low)]
+
+    def either(slot, act_on):
+        @pl.when(slot < extra)
+        def _():
+            act_on(True, share)
+
+        @pl.when(slot >= extra)
+        def _():
+            act_on(False, low)
 
     me_r = rank(me_z, me_h)
     for dz, h in group_m:
         device = at(dz, h, 0, 0)
         slot = rank(device[0] // 2, device[0] % 2)
 
-        @pl.when(slot < owners)
-        def _(device=device, slot=slot):
-            send(pred_send.at[slot], pred_recv.at[me_m], 4, device)
+        def send_pred(more, count, device=device, slot=slot):
+            dst = pred_recv.at[me_m, pl.ds(0, count)]
+            send(tiles_of(pred_send, slot, more), dst, 4, device)
+
+        either(slot, send_pred)
 
     hidden = pre[:, 384:2944]
     gate = jax.nn.sigmoid(hidden)
     pre[:, 384:2944] = gate * (1.0 + hidden * (1.0 - gate))
-    act_own[:, 384:2944] = jnp.where(
-        mask(1, 384, 2944), act[:, 384:2944].astype(F32), 0.0
-    ).astype(BF16)
+    act_t[...] = jnp.where(mask(1, 512, 2816), act[:, 512:2816].astype(F32), 0.0).T.astype(BF16)
+    xc_t[...] = xc[:, 512:2816].astype(F32).T.astype(BF16)
     wait_recv(side_recv.at[1], 2)
     wait_recv(band_recv.at[1], 3)
     unpack(1)
@@ -320,13 +335,14 @@
     def slope(d):
         return d * lax.rsqrt(d * d + 0.25)
 
-    @pl.when(me_r < owners)
-    def _():
-        pred_recv[me_m] = pred_send[me_r]
-        wait_recv(pred_recv.at[pl.ds(0, members - 1)], 4)
-        for u in range(share):
+    def own_tiles(more, count):
+        start = me_r * share if more else extra + me_r * low
+        for u in range(count):
+            pred_recv[me_m, u] = pred_send[start + u]
+        wait_recv(pred_recv.at[pl.ds(0, members - 1), pl.ds(0, count)], 4)
+        for u in range(count):
             everyone = pred_recv[:, u].astype(F32)
-            wanted = target_tiles[me_r + u * owners]
+            wanted = target_tiles[start + u]
             for half in range(2):
                 own = everyone[:, half * 8 : half * 8 + 8]
                 spread = jnp.zeros_like(own)
@@ -340,19 +356,19 @@
             grad_send[:, u] = grads[...].astype(BF16)
         for dz, h in group_m:
             device = at(dz, h, 0, 0)
-            send(grad_send.at[device[0]], grad_recv.at[me_r], 5, device)
-        grad_recv[me_r] = grad_send[me_m]
-        wait_recv(grad_recv.at[pl.ds(0, owners - 1)], 5)
-
-    @pl.when(me_r >= owners)
-    def _():
-        wait_recv(grad_recv, 5)
+            src = grad_send.at[device[0], pl.ds(0, count)]
+            send(src, tiles_of(grad_recv, me_r, more), 5, device)
+        for u in range(count):
+            grad_recv[start + u] = grad_send[me_m, u]
+        wait_recv(grad_recv.at[pl.ds(0, PRED_TILES - count)], 5)
+
+    either(me_r, own_tiles)
 
     for u in range(PRED_TILES):
         t = PRED_FIRST + u
         row, col = place(t * 128, LEV, 128)
         inside = (row >= row_low) & (row < row_high) & (col >= HALO - 2) & (col < HALO + COLS + 2)
-        tile = grad_recv[u % owners, u // owners].astype(F32)
+        tile = grad_recv[u].astype(F32)
         gp[:, t * 128 : t * 128 + 128] = jnp.where(inside, tile, 0.0)
     for k, shift in enumerate(SHIFTS):
         gc[k * LEV : (k + 1) * LEV, 384:2944] = gp[:, 384 - shift : 2944 - shift].astype(BF16)
@@ -381,18 +397,13 @@
             total += ref[i].astype(F32)
         return total
 
-    contract_lanes = (((1,), (1,)), ((), ()))
-    out_part = lax.dot_general(
-        gc[:, 512:2816], act_own[:, 512:2816], contract_lanes, preferred_element_type=F32
-    )
+    out_part = jnp.dot(gc[:, 512:2816], act_t[...], preferred_element_type=F32)
     spread_part(0, out_part)
 
     value = jnp.dot(w_out_t[...], gc[:, 384:2944], preferred_element_type=F32) * pre[:, 384:2944]
     gh_own[:, 384:2944] = jnp.where(mask(1, 384, 2944), value, 0.0).astype(BF16)
     gh[:, 384:2944] = jnp.where(mask(0, 384, 2944), value, 0.0).astype(BF16)
-    in_part = lax.dot_general(
-        xc[:, 512:2816], gh_own[:, 512:2816], contract_lanes, preferred_element_type=F32
-    )
+    in_part = jnp.dot(gh_own[:, 512:2816], xc_t[...], preferred_element_type=F32).T
     spread_part(1, in_part)
 
     taps[:, 384:2944] = jnp.dot(w_in_t[...], gh[:, 384:2944], preferred_element_type=F32)
@@ -403,43 +414,61 @@
             total += taps[k * LEV : (k + 1) * LEV, start - shift : start - shift + COLS]
         by_row[r] = total
 
+    by_lon = (me_o, lons, [at(0, 0, 0, d) for d in group_o])
+    by_z = (me_z, zs, [at(d, 0, 0, 0) for d in group_z])
+    first_axis, second_axis = (by_lon, by_z), (by_z, by_lon)
+
+    def share_sum(value, dst, phase, axis):
+        dst[axis[0]] = value.astype(SUM)
+        for device in axis[2]:
+            send(dst.at[axis[0]], dst.at[axis[0]], phase, device)
+
     for p in range(2):
         wait_recv(part_recv.at[p, pl.ds(0, quads - 1)], 6 + p)
-        lon_recv[me_o, p] = total_of(part_recv.at[p], quads).astype(SUM)
-        others = spare_recv.at[pl.ds(0, quads - 1)]
+        share_sum(total_of(part_recv.at[p], quads), first.at[p], 10 + p, first_axis[p])
 
         @pl.when(me_q == spare_owner[p])
         def _():
             spare_recv[me_q] = part_sum[p, 8]
-            wait_recv(others, 8 + p)
-            lon_recv[me_o, 2] = total_of(spare_recv, quads).astype(SUM)
-
-    for d in group_o:
-        send(lon_recv.at[me_o], lon_recv.at[me_o], 10, at(0, 0, 0, d))
+            wait_recv(spare_recv.at[pl.ds(0, quads - 1)], 8 + p)
+            share_sum(total_of(spare_recv, quads), spare_first, 14, first_axis[p])
+
     for level in range(LEV):
         field[level] = by_row[:, level, :]
-    wait_recv(lon_recv.at[pl.ds(0, lons - 1)], 10)
-    mem_recv[me_z] = total_of(lon_recv, lons).astype(SUM)
-    for d in group_z:
-        send(mem_recv.at[me_z], mem_recv.at[me_z], 11, at(d, 0, 0, 0))
+
+    for p in range(2):
+        count = first_axis[p][1]
+        wait_recv(first.at[p, pl.ds(0, count - 1)], 10 + p)
+        share_sum(total_of(first.at[p], count), second.at[p], 12 + p, second_axis[p])
+
+        @pl.when(me_q == spare_owner[p])
+        def _():
+            wait_recv(spare_first.at[pl.ds(0, count - 1)], 14)
+            share_sum(total_of(spare_first, count), spare_second, 15, second_axis[p])
+
     scale = 1.0 / math.sqrt(members * lats * lons * ROWS * COLS)
-    wait_recv(mem_recv.at[pl.ds(0, zs - 1)], 11)
-    all_recv[me_q] = (total_of(mem_recv, zs) * scale).astype(SUM)
-    for h, da in group_q:
-        send(all_recv.at[me_q], all_recv.at[me_q], 12, at(0, h, da, 0))
+    for p in range(2):
+        count = second_axis[p][1]
+        wait_recv(second.at[p, pl.ds(0, count - 1)], 12 + p)
+        all_recv[p, me_q] = (total_of(second.at[p], count) * scale).astype(SUM)
+        for h, da in group_q:
+            send(all_recv.at[p, me_q], all_recv.at[p, me_q], (16, 19)[p], at(0, h, da, 0))
+
+        @pl.when(me_q == spare_owner[p])
+        def _():
+            wait_recv(spare_second.at[pl.ds(0, count - 1)], 15)
+            spare_all[p] = (total_of(spare_second, count) * scale).astype(SUM)
+            for h, da in group_q:
+                send(spare_all.at[p], spare_all.at[p], 17 + p, at(0, h, da, 0))
 
     for part in range(2):
         wait_send(side_recv.at[part], 2 * part)
         wait_send(band_recv.at[part], 2 * part + 1)
-    @pl.when(me_r < owners)
-    def _():
-        wait_send(pred_send.at[pl.ds(0, owners - 1)], 4)
-        wait_send(grad_send.at[pl.ds(0, members - 1)], 5)
-
-    @pl.when(me_r >= owners)
-    def _():
-        wait_send(pred_send, 4)
-
+    def all_sent(more, count):
+        wait_send(pred_send.at[pl.ds(0, PRED_TILES - count)], 4)
+        wait_send(grad_send.at[pl.ds(0, members - 1), pl.ds(0, count)], 5)
+
+    either(me_r, all_sent)
     for p in range(2):
         wait_send(part_recv.at[p, pl.ds(0, quads - 1)], 6 + p)
 
@@ -447,14 +476,32 @@
         def _():
             wait_send(spare_recv.at[0], 8 + p)
 
-    wait_send(lon_recv.at[pl.ds(0, lons - 1)], 10)
-    wait_send(mem_recv.at[pl.ds(0, zs - 1)], 11)
-    wait_recv(all_recv.at[pl.ds(0, quads - 1)], 12)
     for p in range(2):
-        for t in range(9):
-            value = all_recv[t, p] if t < 8 else all_recv[spare_owner[p], 2]
-            sums_ref[p, t] = value.astype(F32)
-    wait_send(all_recv.at[pl.ds(0, quads - 1)], 12)
+        wait_send(first.at[p, pl.ds(0, first_axis[p][1] - 1)], 10 + p)
+        wait_send(second.at[p, pl.ds(0, second_axis[p][1] - 1)], 12 + p)
+
+        @pl.when(me_q == spare_owner[p])
+        def _():
+            wait_send(spare_first.at[pl.ds(0, first_axis[p][1] - 1)], 14)
+            wait_send(spare_second.at[pl.ds(0, second_axis[p][1] - 1)], 15)
+
+    for p in range(2):
+        wait_recv(all_recv.at[p, pl.ds(0, quads - 1)], (16, 19)[p])
+
+        @pl.when(me_q != spare_owner[p])
+        def _():
+            wait_recv(spare_all.at[p], 17 + p)
+
+        for t in range(8):
+            sums_ref[p, t] = all_recv[p, t].astype(F32)
+        sums_ref[p, 8] = spare_all[p].astype(F32)
+
+    for p in range(2):
+        wait_send(all_recv.at[p, pl.ds(0, quads - 1)], (16, 19)[p])
+
+        @pl.when(me_q == spare_owner[p])
+        def _():
+            wait_send(spare_recv.at[pl.ds(0, quads - 1)], 17 + p)
 
 
 def write_out(field, sums, field_out, gin_out, gout_out, sem):
@@ -473,7 +520,8 @@
 def shards(sizes, inputs, target, conv_in, bias_in, conv_out):
     members, lats, lons = sizes
     quads = 2 * lats
-    share, owners = shares(members)
+    low, extra = shares(members)
+    share = low + 1
     wide = FLAT + LEAD + 128
     anywhere = pl.BlockSpec(memory_space=pl.ANY)
     near = pl.BlockSpec(memory_space=pltpu.VMEM)
@@ -504,14 +552,15 @@
             pltpu.VMEM((TAPS, FLAT), BF16),
             pltpu.VMEM((C, FLAT), F32),
             pltpu.VMEM((C, FLAT), BF16),
-            pltpu.VMEM((C, FLAT), BF16),
+            pltpu.VMEM((2304, C), BF16),
+            pltpu.VMEM((2304, TAPS), BF16),
             pltpu.VMEM((TAPS, FLAT), F32),
-            pltpu.VMEM((owners, share, LEV, 128), BF16),
+            pltpu.VMEM((PRED_TILES, LEV, 128), BF16),
             pltpu.VMEM((members, share, LEV, 128), BF16),
-            pltpu.VMEM((owners * share, LEV, 128), F32),
+            pltpu.VMEM((PRED_TILES, LEV, 128), F32),
             pltpu.VMEM((members, LEV, 128), F32),
             pltpu.VMEM((members, share, LEV, 128), BF16),
-            pltpu.VMEM((owners, share, LEV, 128), BF16),
+            pltpu.VMEM((PRED_TILES, LEV, 128), BF16),
             pltpu.VMEM((LEV, FLAT), F32),
             pltpu.VMEM((TAPS, FLAT), BF16),
             pltpu.VMEM((C, FLAT), BF16),
@@ -520,12 +569,15 @@
             pltpu.VMEM((2, 9, LEV, C), SUM),
             pltpu.VMEM((2, quads, LEV, C), SUM),
             pltpu.VMEM((quads, LEV, C), SUM),
-            pltpu.VMEM((lons, 3, LEV, C), SUM),
-            pltpu.VMEM((members // 2, 3, LEV, C), SUM),
-            pltpu.VMEM((quads, 3, LEV, C), SUM),
+            pltpu.VMEM((2, max(lons, members // 2), LEV, C), SUM),
+            pltpu.VMEM((2, max(lons, members // 2), LEV, C), SUM),
+            pltpu.VMEM((max(lons, members // 2), LEV, C), SUM),
+            pltpu.VMEM((max(lons, members // 2), LEV, C), SUM),
+            pltpu.VMEM((2, LEV, C), SUM),
+            pltpu.VMEM((2, quads, LEV, C), SUM),
             pltpu.SemaphoreType.DMA((5,)),
-            pltpu.SemaphoreType.DMA((13,)),
-            pltpu.SemaphoreType.DMA((13,)),
+            pltpu.SemaphoreType.DMA((20,)),
+            pltpu.SemaphoreType.DMA((20,)),
             pltpu.SemaphoreType.REGULAR((2,)),
         ],
         compiler_params=pltpu.CompilerParams(

time: 51.5 us -> 49.9 us (0.969)
  Pallas kernels: 50.7 us -> 49.1 us
    pallas_call x1, Pallas kernels: 50 us -> 48.4 us  [shards(): pl.pallas_call(functools.partial(kernel, sizes), out_shape=(pltpu.VMEM((L...]
where the time goes in v5:
time: 49.9 us; the launch traced here: 49.8 us
  Pallas kernels  49.1 us (98%)
  between operations  0.64 us (1%)
    pallas_call x1, Pallas kernels, shards(): pl.pallas_call(functools.partial(kernel, sizes), out_shape=(pltpu.VMEM((L...  48.4 us

profile of v5, /device:TPU:1, one launch (start us, length us, event | category | flops | bytes accessed | tf_op | source)
XLA Modules:
  0.0 49.8 jit_solution(4316793545937866202)
XLA Ops:
  0.6 48.4 %downscaling_step.1 = (f32[16,16,128]{2,1,0:T(8,128)S(1)}, f32[2,9,16,128]{3,2,1,0:T(8,128)S(1)}) custom-call(bf16[1,16,16,128]{3,2,1,0:T(8,128)(2,1)} %x_hbm.1, bf16[16,16,128]{2,1,0:T(8,128)(2,1)} %t_hbm.1, bf16[144,128]{1,0:T(8,128)(2,1)} %bitcast.6, f32[1,128]{1,0:T(1,128)} %bitcast.8, bf16[144,128]{1,0:T(8,128)(2,1)} %bitcast.7), custom_call_target="tpu_custom_call" | custom-call | tf_op jit(solution)/shard_map/downscaling_step/pallas_call | solution.py:528
  49.0 0.7 %write_out.1 = (f32[1,16,16,128]{3,2,1,0:T(8,128)}, f32[9,16,128]{2,1,0:T(8,128)}, f32[9,16,128]{2,1,0:T(8,128)}) custom-call(f32[16,16,128]{2,1,0:T(8,128)S(1)} %get-tuple-element.8.field, f32[2,9,16,128]{3,2,1,0:T(8,128)S(1)} %get-tuple-element.9.sums), custom_call_target="tpu_custom_call" | custom-call | tf_op jit(solution)/shard_map/write_out/pallas_call | solution.py:599

commit v6 on v5

--- a/solution.py
+++ b/solution.py
@@ -285,15 +285,14 @@
     act[:, 128:3200] = value
     taps[:, 128:3200] = jnp.dot(w_out[...], value, preferred_element_type=F32)
 
-    for t in range(0, PRED_TILES, 11):
-        begin, width = (PRED_FIRST + t) * 128, 11 * 128
+    def predict(t, count):
+        begin, width = (PRED_FIRST + t) * 128, count * 128
         total = xf[0:LEV, LEAD + begin : LEAD + begin + width]
         for k, shift in enumerate(SHIFTS):
             total += taps[k * LEV : (k + 1) * LEV, begin + shift : begin + shift + width]
-        for u in range(11):
+        for u in range(count):
             pred_send[t + u] = total[:, u * 128 : (u + 1) * 128].astype(BF16)
 
-    hear(1)
     def rank(z, h):
         return ((z + 3) % zs) * 2 + h
 
@@ -311,15 +310,21 @@
             act_on(False, low)
 
     me_r = rank(me_z, me_h)
-    for dz, h in group_m:
-        device = at(dz, h, 0, 0)
-        slot = rank(device[0] // 2, device[0] % 2)
-
-        def send_pred(more, count, device=device, slot=slot):
-            dst = pred_recv.at[me_m, pl.ds(0, count)]
-            send(tiles_of(pred_send, slot, more), dst, 4, device)
-
-        either(slot, send_pred)
+    def send_pred(more):
+        for dz, h in group_m:
+            device = at(dz, h, 0, 0)
+            slot = rank(device[0] // 2, device[0] % 2)
+
+            @pl.when(slot < extra if more else slot >= extra)
+            def _(device=device, slot=slot):
+                dst = pred_recv.at[me_m, pl.ds(0, share if more else low)]
+                send(tiles_of(pred_send, slot, more), dst, 4, device)
+
+    predict(0, extra * share)
+    hear(1)
+    send_pred(True)
+    predict(extra * share, PRED_TILES - extra * share)
+    send_pred(False)
 
     hidden = pre[:, 384:2944]
     gate = jax.nn.sigmoid(hidden)
@@ -354,10 +359,9 @@
                 value = slope(own - wanted[None, half * 8 : half * 8 + 8]) - coupling * spread
                 grads[:, half * 8 : half * 8 + 8, :] = value
             grad_send[:, u] = grads[...].astype(BF16)
-        for dz, h in group_m:
-            device = at(dz, h, 0, 0)
-            src = grad_send.at[device[0], pl.ds(0, count)]
-            send(src, tiles_of(grad_recv, me_r, more), 5, device)
+            for dz, h in group_m:
+                device = at(dz, h, 0, 0)
+                send(grad_send.at[device[0], u], grad_recv.at[start + u], 5, device)
         for u in range(count):
             grad_recv[start + u] = grad_send[me_m, u]
         wait_recv(grad_recv.at[pl.ds(0, PRED_TILES - count)], 5)

time: 49.9 us -> 50.4 us (1.010)
  no operation moved by 1% of the time
where the time goes in v6:
time: 50.4 us; the launch traced here: 50.2 us
  Pallas kernels  49.6 us (98%)
  between operations  0.64 us (1%)
    pallas_call x1, Pallas kernels, shards(): pl.pallas_call(functools.partial(kernel, sizes), out_shape=(pltpu.VMEM((L...  48.9 us

profile of v6, /device:TPU:1, one launch (start us, length us, event | category | flops | bytes accessed | tf_op | source)
XLA Modules:
  0.0 50.2 jit_solution(9773255817615532299)
XLA Ops:
  0.6 48.9 %downscaling_step.1 = (f32[16,16,128]{2,1,0:T(8,128)S(1)}, f32[2,9,16,128]{3,2,1,0:T(8,128)S(1)}) custom-call(bf16[1,16,16,128]{3,2,1,0:T(8,128)(2,1)} %x_hbm.1, bf16[16,16,128]{2,1,0:T(8,128)(2,1)} %t_hbm.1, bf16[144,128]{1,0:T(8,128)(2,1)} %bitcast.6, f32[1,128]{1,0:T(1,128)} %bitcast.8, bf16[144,128]{1,0:T(8,128)(2,1)} %bitcast.7), custom_call_target="tpu_custom_call" | custom-call | tf_op jit(solution)/shard_map/downscaling_step/pallas_call | solution.py:532
  49.5 0.7 %write_out.1 = (f32[1,16,16,128]{3,2,1,0:T(8,128)}, f32[9,16,128]{2,1,0:T(8,128)}, f32[9,16,128]{2,1,0:T(8,128)}) custom-call(f32[16,16,128]{2,1,0:T(8,128)S(1)} %get-tuple-element.8.field, f32[2,9,16,128]{3,2,1,0:T(8,128)S(1)} %get-tuple-element.9.sums), custom_call_target="tpu_custom_call" | custom-call | tf_op jit(solution)/shard_map/write_out/pallas_call | solution.py:603
